TPU v7x, 512 devices: a whole 4x4x16 slice. The times are simulated.
512 devices in a mesh: gx: 16 (over x, z_lo), gy: 8 (over z_hi, core), gz: 4 (over y).
Axes of the slice: x: 4, y: 4, z: 16 (z_hi: 4, z_lo: 4; z = z_hi * 4 + z_lo), core: 2. Of those that a mesh axis runs over, the one named last changes fastest.
Arguments:
- coarse: float32 [16, 32, 16, 128], P(None, 'gx', 'gy', 'gz'), may hold values from -6 to 6
- cotangent: float32 [16, 128, 64, 512], P(None, 'gx', 'gy', 'gz'), may hold values from -6 to 6
- edge_in: float32 [16, 35], replicated, may hold values from -1 to 1
- edge_out: float32 [16, 16], replicated, may hold values from -1.5 to 1.5
- node_in: float32 [16, 32], replicated, may hold values from -1 to 1
- node_out: float32 [16, 16], replicated, may hold values from -1.5 to 1.5
- biases: float32 [3, 16], replicated, may hold values from -3 to 3
Outputs:
- grad_coarse: float32 [16, 32, 16, 128], P(None, 'gx', 'gy', 'gz')
- grad_edge_in: float32 [16, 35], replicated
- grad_edge_out: float32 [16, 16], replicated
- grad_node_in: float32 [16, 32], replicated
- grad_node_out: float32 [16, 16], replicated
- grad_biases: float32 [3, 16], replicated
All inputs are finite; a program needn't handle non-finite values.
Results may differ from a plain program's by a relative error of at most 0.00023.
Values sent between devices are 32-bit elements; how exact they have to be, the bound alone decides.
A program may use at most 64 MiB of HBM per device.

v0:
```python
import jax
import jax.numpy as jnp
import numpy as np
from jax import lax
from jax.experimental import pallas as pl
from jax.experimental.pallas import tpu as pltpu
from jax.sharding import PartitionSpec as P

MESH = pl.DeviceIdType.MESH
F32 = jnp.float32
BF16 = jnp.bfloat16
T = np.array(
    [
        -1.0,
        -0.8717401485096066,
        -0.5917001814331423,
        -0.2092992179024789,
        0.2092992179024789,
        0.5917001814331423,
        0.8717401485096066,
        1.0,
    ]
)
L0, L1 = (1.0 - T) / 2.0, (1.0 + T) / 2.0
LOG2E = float(np.log2(np.e))
LN2 = float(np.log(2.0))
GAP_UP = [float(T[i + 1] - T[i]) if i < 7 else float(T[1] - T[0]) for i in range(8)]
GAP_DOWN = [float(T[i - 1] - T[i]) if i > 0 else float(T[6] - T[7]) for i in range(8)]
Z_LOW = 4
CORES = 2
ABSENT = -1.0e5
SLOT = {0: 0, 1: 1, -1: 2, 2: 3}
STEPS = (-2, -1, 1, 2)

RZ, RZ_UP, RZ_DOWN, PROFILES, Y_STD, Y_NEXT, Y_GAP, DELTA = 0, 32, 64, 96, 136, 168, 296, 328
TABLE_ROWS = 376


def make_table():
    table = np.zeros((TABLE_ROWS, 128))
    for lane in range(128):
        e, a = divmod(lane, 8)
        table[RZ + e + 1, lane] += L0[a]
        table[RZ + e + 2, lane] += L1[a]
        if a < 7:
            table[RZ_UP + e + 1, lane] += L0[a + 1]
            table[RZ_UP + e + 2, lane] += L1[a + 1]
        else:
            table[RZ_UP + e + 2, lane] += L0[1]
            table[RZ_UP + e + 3, lane] += L1[1]
        if a > 0:
            table[RZ_DOWN + e + 1, lane] += L0[a - 1]
            table[RZ_DOWN + e + 2, lane] += L1[a - 1]
        else:
            table[RZ_DOWN + e, lane] += L0[6]
            table[RZ_DOWN + e + 1, lane] += L1[6]
        table[RZ_UP + 20, lane] = GAP_UP[a]
        table[RZ_DOWN + 20, lane] = GAP_DOWN[a]
    up = np.zeros((4, 8))
    down = np.zeros((4, 8))
    for y in range(8):
        if y < 7:
            up[1, y], up[2, y] = L0[y + 1], L1[y + 1]
        else:
            up[2, y], up[3, y] = L0[1], L1[1]
        if y > 0:
            down[1, y], down[2, y] = L0[y - 1], L1[y - 1]
        else:
            down[0, y], down[1, y] = L0[6], L1[6]
    for i, profile in enumerate((L1, up[2], up[3], down[2], down[0])):
        table[PROFILES + 8 * i : PROFILES + 8 * i + 8] = profile[:, None]
    for c in range(16):
        for y in range(8):
            lane = 8 * c + y
            table[Y_STD + c, lane] = L0[y]
            table[Y_STD + 16 + c, lane] = L1[y]
            for q in range(4):
                table[Y_NEXT + 16 * q + c, lane] = up[q, y]
                table[Y_NEXT + 64 + 16 * q + c, lane] = down[q, y]
            table[Y_GAP + c, lane] = GAP_UP[y]
            table[Y_GAP + 16 + c, lane] = GAP_DOWN[y]
            table[DELTA + c, lane] = 1.0
            table[DELTA + 16 + c, lane] = 1.0 if y == 0 else 0.0
            table[DELTA + 32 + c, lane] = 1.0 if y == 7 else 0.0
    return table.astype(np.float32)


NN = (((1,), (0,)), ((), ()))
NT = (((1,), (1,)), ((), ()))


def dot(a, b, dims=NN):
    return lax.dot_general(a, b, dims, preferred_element_type=F32)


def split(a):
    high = a.astype(BF16)
    return high, (a - high.astype(F32)).astype(BF16)


def mm(a, b, dims=NN):
    (ah, al), (bh, bl) = a, b
    return dot(ah, bh, dims) + (dot(ah, bl, dims) + dot(al, bh, dims))


def mm_exact(a, b, dims=NN):
    return dot(a[0], b, dims) + dot(a[1], b, dims)


def exact_mm(a, b, dims=NN):
    return dot(a, b[0], dims) + dot(a, b[1], dims)


def iota(shape, dim):
    return lax.broadcasted_iota(jnp.int32, shape, dim)


def ones_where(mask):
    return jnp.where(mask, 1.0, 0.0).astype(F32)


def spread(a, k):
    k = k % 4
    return a if k == 0 else pltpu.roll(a, 32 * k, 1)


def vertex_maps():
    row, col = iota((128, 128), 0), iota((128, 128), 1)
    layer, vertex = row % 32, col % 32 - 1
    same = (row // 32 == col // 32) & (vertex < 18)
    maps = []
    for shift in (0, 16, -16):
        v = vertex + shift
        maps.append(ones_where(same & ((layer == 2 * v - 1) | (layer == 2 * v))).astype(BF16))
    return maps


def make_main(sizes):
    n_x, n_y, n_z = sizes
    z_high = n_y // CORES
    n_layers = z_high * Z_LOW
    n_cols = n_x // Z_LOW
    n_plane = n_cols * n_z

    def kernel(
        coarse, cot_hbm, edge_in, edge_out, node_in, node_out, biases, table,
        out,
        cot, p0, zr, tb, xr, vx, yr, means, lhs_rows, rows, e_all, e_sum, s_all, hn_all, u_all, g_all, xf,
        gm, yb, gy_all, xb, gx_all, zb, payload, core_slot, col_slots, plane_slots, total,
        cot_sem, zf_s, zf_r, xf_s, xf_r, yf_s, yf_r, yb_s, yb_r, xb_s, xb_r, zb_s, zb_r,
        core_s, core_r, col_s, col_r, plane_s, plane_r, cast_s, cast_r,
    ):
        ix, iy, iz = lax.axis_index("gx"), lax.axis_index("gy"), lax.axis_index("gz")
        low = lax.rem(ix, Z_LOW)
        core = lax.rem(iy, CORES)
        layer = (iy // CORES) * Z_LOW + low
        on_core0 = core == 0
        is_root = on_core0 & (layer == 0)
        is_leaf = on_core0 & (layer != 0)

        def at_x(d):
            return (lax.rem(ix + (d + n_x), n_x), iy, iz)

        def at_y(d):
            return (ix, lax.rem(iy + (d + n_y), n_y), iz)

        def at_z(d):
            return (ix, iy, lax.rem(iz + (d + n_z), n_z))

        sibling = (ix, iy + 1 - 2 * core, iz)
        column_root = (ix - low, 0, iz)

        def in_column(k, c):
            return (ix + k % Z_LOW, (k // Z_LOW) * CORES + c, iz)

        def in_plane(k):
            col, row = k // n_z, k % n_z
            return (lax.rem(ix + Z_LOW * col, n_x), iy, lax.rem(iz + row, n_z))

        def send(src, dst, send_sem, recv_sem, device):
            return pltpu.make_async_remote_copy(
                src_ref=src, dst_ref=dst, send_sem=send_sem, recv_sem=recv_sem, device_id=device, device_id_type=MESH
            )

        def signal(device):
            pl.semaphore_signal(barrier, inc=1, device_id=device, device_id_type=MESH)

        load_cot = pltpu.make_async_copy(cot_hbm, cot, cot_sem)
        load_cot.start()
        barrier = pltpu.get_barrier_semaphore()
        for d in (-1, 1):
            signal(at_z(d))
        for d in STEPS:
            signal(at_x(d))
        for d in STEPS:
            signal(at_y(d))

        @pl.when(layer != 0)
        def _():
            signal(column_root)

        @pl.when(is_root)
        def _():
            for k in range(1, n_layers):
                signal(in_column(k, 0))
            for k in range(1, n_plane):
                signal(in_plane(k))

        expected = 10 + jnp.where(is_leaf, 1, 0) + jnp.where(is_root, CORES * (n_layers - 1) + n_plane - 1, 0)

        block = coarse[...]
        p0[...] = jnp.concatenate([block[:, p, q, :] for q in (0, 1) for p in (0, 1)], axis=1)
        pl.semaphore_wait(barrier, expected)

        z_sends = [
            send(p0, zr.at[0], zf_s.at[0], zf_r.at[0], at_z(1)),
            send(p0, zr.at[1], zf_s.at[1], zf_r.at[1], at_z(-1)),
        ]
        for c in z_sends:
            c.start()

        w_own, w_other = edge_in[:, 0:16], edge_in[:, 16:32]
        col_x, col_y, col_z = edge_in[:, 32:33], edge_in[:, 33:34], edge_in[:, 34:35]
        n_own, n_gathered = node_in[:, 0:16], node_in[:, 16:32]
        eye = ones_where(iota((16, 16), 0) == iota((16, 16), 1)).astype(BF16)
        delta = table[DELTA : DELTA + 16, :].astype(BF16)
        same_y = iota((128, 128), 0) % 8 == iota((128, 128), 1) % 8

        def transposed(w):
            return exact_mm(eye, split(w), NT)

        def widen(w):
            parts = []
            for part in split(w):
                left = dot(delta, part, (((0,), (0,)), ((), ()))).astype(BF16)
                parts.append(jnp.where(same_y, dot(left, delta), 0.0).astype(BF16))
            return tuple(parts)

        m1 = mm(split(n_gathered), split(edge_out[...]))
        m1_wide = widen(m1)
        m1_back = widen(transposed(m1))
        out_back = widen(transposed(node_out[...]))
        mix = split(jnp.concatenate([w_own, n_own, w_other], axis=0))
        mix_back = split(jnp.concatenate([transposed(n_own), transposed(w_own), transposed(w_other)], axis=1))
        bias_rows = biases[...]
        bias_cols = exact_mm(eye, split(bias_rows), NT)
        b0_col, b1_row, b2_col = bias_cols[:, 0:1], bias_rows[1:2, :], bias_cols[:, 2:3]
        nb_col = jnp.sum(n_gathered * b1_row, axis=1, keepdims=True)
        maps = vertex_maps()
        lane = iota((16, 128), 1)
        group, place = lane // 32, lane % 32
        gap_lane = ones_where((place == 20) & (group < 2))

        def blocks4(first):
            t = table[first : first + 32, :]
            zero = jnp.zeros((32, 128), F32)
            return split(
                jnp.concatenate(
                    [jnp.concatenate([t if i == j else zero for j in range(4)], axis=1) for i in range(4)], axis=0
                )
            )

        rz, rz_up, rz_down = blocks4(RZ), blocks4(RZ_UP), blocks4(RZ_DOWN)

        z_sends[0].wait_recv()
        z_sends[1].wait_recv()
        tb[...] = (
            mm_exact(split(p0[...]), maps[0])
            + mm_exact(split(zr[0]), maps[1])
            + mm_exact(split(zr[1]), maps[2])
        )
        x_sends = []
        for d in STEPS:
            i = STEPS.index(-d)
            x_sends.append(send(tb, xr.at[i], xf_s.at[i], xf_r.at[i], at_x(d)))
        for c in x_sends:
            c.start()

        load_cot.wait()
        for k in range(4):
            wide = jnp.concatenate([cot[:, 2 * k + i].reshape(128, 128) for i in (0, 1)], axis=1)
            u_all[:, :, 256 * k : 256 * k + 256] = mm(out_back, split(wide)).reshape(16, 8, 256)
        sum_all, sum_one = cot[:, 0], jnp.zeros((16, 8, 128), F32)
        for x in range(1, 8):
            sum_all = sum_all + cot[:, x]
            sum_one = sum_one + float(L1[x]) * cot[:, x]
        xf[:, :, 0:128] = sum_all - sum_one
        xf[:, :, 128:256] = sum_one

        for c in x_sends:
            c.wait_recv()
        x_blocks = {0: tb[...]}
        for i, d in enumerate(STEPS):
            x_blocks[d] = xr[i]
        for q in (0, 1):
            acc = jnp.zeros((16, 128), F32)
            for vertex in (-1, 0, 1, 2):
                for d in (vertex - 1, vertex):
                    moved = spread(x_blocks[d], SLOT[vertex] - (2 * q + vertex - d))
                    acc = acc + jnp.where(group == SLOT[vertex], moved, 0.0)
            vx[q] = acc
        y_sends = []
        for d in STEPS:
            i = STEPS.index(-d)
            qs = pl.ds(0, 2) if abs(d) == 1 else pl.ds(1 if d == 2 else 0, 1)
            y_sends.append(send(vx.at[qs], yr.at[i, qs], yf_s.at[i], yf_r.at[i], at_y(d)))
        for c in y_sends:
            c.start()

        def exists(d):
            return jnp.where((iy + d >= 0) & (iy + d < n_y), 1.0, 0.0).astype(F32)

        there = {d: exists(d) for d in (-2, -1, 0, 1, 2)}
        wall_low, wall_high = 1.0 - there[-1], 1.0 - there[1]
        y_index = iota((8, 128), 0)
        count = 6.0 - wall_low * ones_where(y_index == 0) - wall_high * ones_where(y_index == 7)
        ly, up1, up2, down1, down0 = (table[PROFILES + 8 * i : PROFILES + 8 * i + 8, :] for i in range(5))

        for c in y_sends:
            c.wait_recv()

        def y_block(d, q):
            return vx[q] if d == 0 else yr[STEPS.index(d), q] * there[d]

        for q in (-1, 0, 1, 2):
            copies = jnp.maximum(there[q - 1] + there[q], 1.0)
            means[q + 1] = (y_block(q - 1, 1) + y_block(q, 0)) * (0.25 / copies)

        mixed = mm(mix, split(jnp.concatenate([means[i] for i in range(4)], axis=1)))
        for i in range(4):
            lanes = slice(128 * i, 128 * i + 128)
            if i in (1, 2):
                lhs_rows[48 * (i - 1) : 48 * (i - 1) + 32, :] = mixed[0:32, lanes]
                lhs_rows[48 * (i - 1) + 32 : 48 * i, :] = mixed[32:48, lanes] + col_z * gap_lane
            else:
                first = 96 if i == 0 else 112
                lhs_rows[first : first + 16, :] = mixed[32:48, lanes]
        along = mm(split(lhs_rows[...]), rz)
        other01 = split(jnp.concatenate([lhs_rows[32:48, :], lhs_rows[80:96, :]], axis=0))
        along_up = mm(other01, (rz_up[0][:, 0:256], rz_up[1][:, 0:256]))
        along_down = mm(other01, (rz_down[0][:, 0:256], rz_down[1][:, 0:256]))

        def vertex_rows(field, q, vertex):
            first = {0: 0, 1: 48}[q] + 16 * field if q in (0, 1) else (96 if q == -1 else 112)
            s = SLOT[vertex]
            return along[first : first + 16, 128 * s : 128 * s + 128]

        def next_rows(source, q, vertex):
            return source[16 * q : 16 * q + 16, 128 * vertex : 128 * vertex + 128]

        def put(field, x, value):
            rows[pl.ds(128 * field + x, 16, stride=8), :] = value

        def line(a, b, t):
            return a + t * (b - a)

        for x in range(8):
            t = float(L1[x])
            here = float(T[x]) * col_x
            own = [
                (line(vertex_rows(0, q, 0), vertex_rows(0, q, 1), t) + (b0_col - here - (2 * q - 1.0) * col_y)) * LOG2E
                for q in (0, 1)
            ]
            put(0, x, own[0])
            put(1, x, own[1] - own[0])
            other = {
                q: (line(vertex_rows(2, q, 0), vertex_rows(2, q, 1), t) + (here + (2 * q - 1.0) * col_y)) * LOG2E
                for q in (-1, 0, 1, 2)
            }
            put(2, x, other[0])
            put(3, x, other[1] - other[0])
            put(5, x, (other[2] - other[0]) * there[1] + ABSENT * wall_high)
            put(6, x, (other[-1] - other[0]) * there[-1] + ABSENT * wall_low)
            for f, source in ((7, along_up), (9, along_down)):
                z = [
                    (line(next_rows(source, q, 0), next_rows(source, q, 1), t) + (here + (2 * q - 1.0) * col_y)) * LOG2E
                    for q in (0, 1)
                ]
                put(f, x, z[0])
                put(f + 1, x, z[1] - z[0])
            hn = [line(vertex_rows(1, q, 0), vertex_rows(1, q, 1), t) for q in (0, 1)]
            put(11, x, hn[0] + b2_col)
            put(12, x, hn[1] - hn[0])
            put(13, x, jnp.broadcast_to(nb_col, (16, 128)))
        for side, (a, b, t, at) in enumerate(((-1, 0, float(L1[6]), float(T[6]) - 2.0), (1, 2, float(L1[1]), float(T[1]) + 2.0))):
            other = [
                (line(vertex_rows(2, q, a), vertex_rows(2, q, b), t) + (at * col_x + (2 * q - 1.0) * col_y)) * LOG2E
                for q in (0, 1)
            ]
            put(4, 2 * side, other[0])
            put(4, 2 * side + 1, other[1] - other[0])

        def forward(c, carry):
            def row(field, x):
                return rows[pl.ds(128 * field + 8 * c + x, 1), :]

            other = [row(4, 0) + ly * row(4, 1)]
            for x in range(8):
                other.append(row(2, x) + ly * row(3, x))
            other.append(row(4, 2) + ly * row(4, 3))
            for x in range(8):
                own = row(0, x) + ly * row(1, x)
                a, d = row(2, x), row(3, x)
                senders = (
                    other[x + 2],
                    other[x],
                    a + up1 * d + up2 * row(5, x),
                    a + down1 * d + down0 * row(6, x),
                    row(7, x) + ly * row(8, x),
                    row(9, x) + ly * row(10, x),
                )
                tops, decays = None, None
                for k, sender in enumerate(senders):
                    z = own + sender
                    decay = jnp.exp2(jnp.minimum(z, 0.0))
                    top = jnp.maximum(z, 0.0)
                    e_all[k, x, c] = decay
                    tops = top if tops is None else tops + top
                    decays = decay if decays is None else decays + decay
                e_sum[x, c] = decays
                s_all[c, :, 128 * x : 128 * x + 128] = LN2 * tops + (decays - count)
                hn_all[c, :, 128 * x : 128 * x + 128] = row(11, x) + ly * row(12, x) + count * row(13, x)
            return carry

        lax.fori_loop(0, 16, forward, 0)

        outer_out = jnp.zeros((128, 128), F32)
        outer_in = jnp.zeros((128, 128), F32)
        dh_all = jnp.zeros((16, 8, 128), F32)
        dh_one = jnp.zeros((16, 8, 128), F32)
        for k in range(4):
            lanes = slice(256 * k, 256 * k + 256)
            s = split(s_all[:, :, lanes].reshape(128, 256))
            h = mm(m1_wide, s) + hn_all[:, :, lanes].reshape(128, 256)
            decay = jnp.exp(jnp.minimum(h, 0.0))
            a = jnp.maximum(h, 0.0) + (decay - 1.0)
            dh = decay * u_all[:, :, lanes].reshape(128, 256)
            dh_parts = split(dh)
            g_all[:, :, lanes] = mm(m1_back, dh_parts).reshape(16, 8, 256)
            wide = jnp.concatenate([cot[:, 2 * k + i].reshape(128, 128) for i in (0, 1)], axis=1)
            outer_out = outer_out + mm(split(wide), split(a), NT)
            outer_in = outer_in + mm(dh_parts, s, NT)
            for i in (0, 1):
                part = dh[:, 128 * i : 128 * i + 128].reshape(16, 8, 128)
                dh_all = dh_all + part
                dh_one = dh_one + float(L1[2 * k + i]) * part
        xf[:, :, 256:384] = dh_all - dh_one
        xf[:, :, 384:512] = dh_one

        def backward(c, carry):
            g = [g_all[c, :, 128 * x : 128 * x + 128] for x in range(8)]
            own = [g[x] * e_sum[x, c] for x in range(8)]

            def bz(k, x):
                return g[x] * e_all[k, x, c]

            def save(i, value):
                xf[c, :, 128 * i : 128 * i + 128] = value

            def reduce(first, values):
                everything, one = values[0], float(L1[1]) * values[1]
                for x in range(1, 8):
                    everything = everything + values[x]
                for x in range(2, 8):
                    one = one + float(L1[x]) * values[x]
                save(first, everything - one)
                save(first + 1, one)

            reduce(4, own)
            ups = [bz(0, x) for x in range(8)]
            downs = [bz(1, x) for x in range(8)]
            acc = GAP_UP[0] * ups[0] + GAP_DOWN[0] * downs[0]
            for x in range(1, 8):
                acc = acc + GAP_UP[x] * ups[x] + GAP_DOWN[x] * downs[x]
            save(6, acc)
            at = [downs[1]] + [ups[x - 1] + downs[x + 1] for x in range(1, 7)] + [ups[6]]
            everything, one = at[0], float(L1[1]) * at[1]
            for x in range(1, 8):
                everything = everything + at[x]
            for x in range(2, 8):
                one = one + float(L1[x]) * at[x]
            save(7, everything - one + float(L1[6]) * downs[0])
            save(8, one + float(L0[1]) * ups[7])
            save(9, float(L0[6]) * downs[0])
            save(10, float(L1[1]) * ups[7])
            for k in range(4):
                reduce(11 + 2 * k, [bz(2 + k, x) for x in range(8)])
            return carry

        lax.fori_loop(0, 16, backward, 0)

        def along_z(first, n, by):
            return mm(
                split(xf[:, :, 128 * first : 128 * (first + n)].reshape(128, 128 * n)),
                (by[0][:, 0 : 128 * n], by[1][:, 0 : 128 * n]),
                NT,
            )

        z1 = along_z(0, 4, rz)
        z2 = along_z(4, 3, rz)
        z3 = along_z(7, 4, rz) + along_z(15, 2, rz_up) + along_z(17, 2, rz_down)
        z4 = along_z(11, 4, rz)
        counting = (
            6.0 * table[DELTA : DELTA + 16, :]
            - wall_low * table[DELTA + 16 : DELTA + 32, :]
            - wall_high * table[DELTA + 32 : DELTA + 48, :]
        )
        left = split(jnp.concatenate([table[Y_STD : Y_STD + 32, :], counting], axis=0))
        std = mm(left, split(jnp.concatenate([z1, z2, z3], axis=1)))
        nxt = mm(split(table[Y_NEXT : Y_NEXT + 160, :]), split(z4))

        low_half, low_lanes = group < 2, ones_where(group < 2)
        fields = {}
        for q in (0, 1):
            r = slice(16 * q, 16 * q + 16)
            fields[q] = (std[r, 0:128], std[r, 128:256], std[r, 256:384])
        others = {}
        for q in (-1, 0, 1, 2):
            r_up = slice(16 * (q + 1), 16 * (q + 1) + 16)
            r_down = slice(64 + 16 * (q + 1), 64 + 16 * (q + 1) + 16)
            both = jnp.where(low_half, nxt[r_up, :] + pltpu.roll(nxt[r_down, :], 64, 1), 0.0)
            others[q] = both + fields[q][2] if q in (0, 1) else both

        zero = jnp.zeros((16, 128), F32)
        stacked = []
        for q in (-1, 0, 1, 2):
            if q in (0, 1):
                dh_q = jnp.where(low_half, pltpu.roll(fields[q][0], 64, 1), 0.0)
                own_q = jnp.where(low_half, fields[q][1], 0.0)
            else:
                dh_q, own_q = zero, zero
            stacked.append(jnp.concatenate([dh_q, own_q, others[q]], axis=0))
        back = mm(mix_back, split(jnp.concatenate(stacked, axis=1)))
        for q in (-1, 0, 1, 2):
            value = back[:, 128 * (q + 1) : 128 * (q + 2)]
            if q in (0, 1):
                value = value + jnp.where(low_half, fields[q][0], 0.0)
            gm[q + 1] = value
        y_back = []
        for d in STEPS:
            i = STEPS.index(-d)
            if abs(d) == 1:
                src, dst = gm.at[pl.ds(2 if d == 1 else 0, 2)], yb.at[i]
            else:
                src, dst = gm.at[pl.ds(3 if d == 2 else 0, 1)], yb.at[i, pl.ds(0 if d == 2 else 1, 1)]
            y_back.append(send(src, dst, yb_s.at[i], yb_r.at[i], at_y(d)))
        for c in y_back:
            c.start()

        summed_out = jnp.where(same_y, outer_out, 0.0)
        summed_in = jnp.where(same_y, outer_in, 0.0)
        big = exact_mm(delta, split(jnp.concatenate([summed_out, summed_in], axis=1)))
        r2, c2 = iota((128, 256), 0), iota((128, 256), 1)
        placing = ones_where((c2 // 128 * 16 + c2 % 128 // 8) == r2).astype(BF16)
        part = mm_exact(split(big), placing, NT)
        r8, l8 = iota((8, 128), 0), iota((8, 128), 1)

        def marked(r, mask):
            return ones_where((r8 == r) & mask)

        def right(first, rows16, special):
            pieces = []
            if rows16 is None:
                pieces.append(jnp.zeros((80, 128), F32))
            else:
                if first > 0:
                    pieces.append(jnp.zeros((first, 128), F32))
                pieces.append(rows16)
                if first < 64:
                    pieces.append(jnp.zeros((64 - first, 128), F32))
            pieces += [special, jnp.zeros((40, 128), F32)]
            return jnp.concatenate(pieces, axis=0)

        lefts, rights = [], []
        none8 = jnp.zeros((8, 128), F32)
        for q in (-1, 0, 1, 2):
            m = means[q + 1]
            if q in (0, 1):
                lefts.append(fields[q][0])
                rights.append(right(32, jnp.where(low_half, 0.0, pltpu.roll(m, 64, 1)), marked(4, l8 >= 64)))
                lefts.append(fields[q][1])
                rights.append(right(48, m * low_lanes, marked(3, l8 < 64) + marked(0, (l8 >= 64) & (l8 < 96))))
            lefts.append(others[q])
            rights.append(right(64, m, marked(2, (l8 % 32 == 20) & (l8 < 64)) if q in (0, 1) else none8))
        lefts += [std[32:48, 0:128], nxt[128:144, :], nxt[144:160, :]]
        rights += [
            right(0, None, marked(5, l8 >= 64)),
            right(0, None, marked(1, l8 < 64)),
            right(0, None, marked(1, l8 >= 64)),
        ]
        payload[...] = part + mm(split(jnp.concatenate(lefts, axis=1)), split(jnp.concatenate(rights, axis=1)), NT)

        to_core0 = send(payload, core_slot, core_s, core_r, sibling)
        to_root = send(payload, col_slots.at[jnp.maximum(layer - 1, 0)], col_s, col_r.at[jnp.maximum(layer - 1, 0)], column_root)

        @pl.when(core == 1)
        def _():
            to_core0.start()

        @pl.when(on_core0)
        def _():
            to_core0.wait_recv()
            payload[...] = payload[...] + core_slot[...]

        @pl.when(is_leaf)
        def _():
            to_root.start()

        for c in y_back:
            c.wait_recv()
        for q in (0, 1):
            value = gm[q + 1]
            for d in (-2, -1, 1, 2):
                if (d, q) not in ((-2, 1), (2, 0)):
                    value = value + yb[STEPS.index(d), q] * there[d]
            gy_all[q] = value
        x_back = []
        for d in STEPS:
            i = STEPS.index(-d)
            x_back.append(send(gy_all, xb.at[i], xb_s.at[i], xb_r.at[i], at_x(d)))
        for c in x_back:
            c.start()

        my_place = (ix // Z_LOW) * n_z + iz
        to_plane = [
            send(plane_slots.at[my_place], plane_slots.at[my_place], plane_s.at[k], plane_r.at[k], in_plane(k))
            for k in range(1, n_plane)
        ]

        @pl.when(is_root)
        def _():
            value = payload[...]
            for k in range(n_layers - 1):
                send(payload, col_slots.at[k], col_s, col_r.at[k], in_column(k + 1, 0)).wait_recv()
                value = value + col_slots[k]
            plane_slots[my_place] = value
            for c in to_plane:
                c.start()

        for c in x_back:
            c.wait_recv()
        for q in (0, 1):
            value = gy_all[q]
            for d in (-2, -1, 1, 2):
                for p in (0, 1):
                    vertex = p - d
                    if vertex in SLOT:
                        moved = spread(xb[STEPS.index(d), q], p - SLOT[vertex])
                        value = value + jnp.where(group == p, moved, 0.0)
            gx_all[q] = jnp.where(low_half, value, 0.0)
        z_back = [
            send(gx_all, zb.at[0], zb_s.at[0], zb_r.at[0], at_z(1)),
            send(gx_all, zb.at[1], zb_s.at[1], zb_r.at[1], at_z(-1)),
        ]
        for c in z_back:
            c.start()

        to_all = [
            send(total, total, cast_s.at[CORES * k + c], cast_r, in_column(k, c))
            for k in range(n_layers)
            for c in range(CORES)
            if (k, c) != (0, 0)
        ]

        @pl.when(is_root)
        def _():
            for k, c in enumerate(to_plane):
                c.wait_recv()
            value = plane_slots[0]
            for k in range(1, n_plane):
                value = value + plane_slots[k]
            total[...] = value
            for c in to_all:
                c.start()

        for c in z_back:
            c.wait_recv()
        for q in (0, 1):
            value = (
                mm_exact(split(gx_all[q]), maps[0], NT)
                + mm_exact(split(zb[0, q]), maps[2], NT)
                + mm_exact(split(zb[1, q]), maps[1], NT)
            )
            neighbour = there[-1] if q == 0 else there[1]
            out[16 * q : 16 * q + 16, :] = value * (0.25 / (1.0 + neighbour))

        @pl.when(jnp.logical_not(is_root))
        def _():
            to_all[0].wait_recv()

        out[32:48, :] = total[...]

        for c in z_sends + x_sends + y_sends + y_back + x_back + z_back:
            c.wait_send()

        @pl.when(core == 1)
        def _():
            to_core0.wait_send()

        @pl.when(is_leaf)
        def _():
            to_root.wait_send()

        @pl.when(is_root)
        def _():
            for c in to_plane + to_all:
                c.wait_send()

    block = pltpu.VMEM((16, 128), F32)

    def blocks(*lead):
        return pltpu.VMEM(lead + (16, 128), F32)

    dma = pltpu.SemaphoreType.DMA
    scratch = [
        pltpu.VMEM((16, 8, 8, 128), F32),
        block,
        blocks(2),
        block,
        blocks(4),
        blocks(2),
        blocks(4, 2),
        blocks(4),
        pltpu.VMEM((128, 128), F32),
        pltpu.VMEM((14 * 128, 128), F32),
        pltpu.VMEM((6, 8, 16, 8, 128), F32),
        pltpu.VMEM((8, 16, 8, 128), F32),
        pltpu.VMEM((16, 8, 1024), F32),
        pltpu.VMEM((16, 8, 1024), F32),
        pltpu.VMEM((16, 8, 1024), F32),
        pltpu.VMEM((16, 8, 1024), F32),
        pltpu.VMEM((16, 8, 19 * 128), F32),
        blocks(4),
        blocks(4, 2),
        blocks(2),
        blocks(4, 2),
        blocks(2),
        blocks(2, 2),
        block,
        block,
        blocks(n_layers - 1),
        blocks(n_plane),
        block,
        dma,
        dma((2,)), dma((2,)), dma((4,)), dma((4,)), dma((4,)), dma((4,)),
        dma((4,)), dma((4,)), dma((4,)), dma((4,)), dma((2,)), dma((2,)),
        dma, dma, dma, dma((n_layers - 1,)), dma((n_plane,)), dma((n_plane,)), dma((CORES * n_layers,)), dma,
    ]
    vmem = pl.BlockSpec(memory_space=pltpu.VMEM)
    return pl.pallas_call(
        kernel,
        out_shape=jax.ShapeDtypeStruct((48, 128), F32),
        in_specs=[vmem, pl.BlockSpec(memory_space=pl.ANY)] + [vmem] * 6,
        out_specs=vmem,
        scratch_shapes=scratch,
        compiler_params=pltpu.CompilerParams(
            collective_id=0, has_side_effects=True, vmem_limit_bytes=40 * 1024 * 1024
        ),
    )


def make_finish(factor):
    def kernel(packed, edge_out, node_in, biases, grad_coarse, g_edge_in, g_edge_out, g_node_in, g_node_out, g_biases):
        for q in (0, 1):
            block = packed[16 * q : 16 * q + 16, :]
            for p in (0, 1):
                grad_coarse[:, p, q, :] = block[:, 32 * p : 32 * p + 32]
        total = packed[32:48, :] * factor
        g_node_out[...] = total[:, 0:16]
        g_edge_in[...] = total[:, 48:83]
        n_gathered = node_in[:, 16:32]
        eye = ones_where(iota((16, 16), 0) == iota((16, 16), 1)).astype(BF16)
        n_back = exact_mm(eye, split(n_gathered), NT)
        back = mm(split(n_back), split(total))
        g_edge_out[...] = back[:, 16:32]
        outer_in = total[:, 16:32]
        g_node_in[:, 0:16] = total[:, 32:48]
        g_node_in[:, 16:32] = mm(split(outer_in), split(edge_out[...]), NT) + total[:, 85:86] * biases[1:2, :]
        rows = jnp.concatenate([total, back], axis=1)
        r, c = iota((8, 256), 0), iota((8, 256), 1)
        pick = ones_where(((r == 0) & (c == 83)) | ((r == 1) & (c == 128 + 85)) | ((r == 2) & (c == 84))).astype(BF16)
        g_biases[...] = exact_mm(pick, split(rows), NT)[0:3, :]

    vmem = pl.BlockSpec(memory_space=pltpu.VMEM)
    shapes = ((16, 2, 2, 32), (16, 35), (16, 16), (16, 32), (16, 16), (3, 16))
    return pl.pallas_call(
        kernel,
        out_shape=[jax.ShapeDtypeStruct(s, F32) for s in shapes],
        in_specs=[vmem] * 4,
        out_specs=[vmem] * 6,
    )


def solution(mesh):
    sizes = (mesh.shape["gx"], mesh.shape["gy"], mesh.shape["gz"])
    table = make_table()

    def on_device(coarse, cotangent, edge_in, edge_out, node_in, node_out, biases):
        nodes = cotangent.shape[1] * cotangent.shape[2] * cotangent.shape[3] * sizes[0] * sizes[1] * sizes[2]
        packed = make_main(sizes)(
            coarse, cotangent, edge_in, edge_out, node_in, node_out, biases, jnp.asarray(table)
        )
        return tuple(make_finish(float(nodes) ** -0.5)(packed, edge_out, node_in, biases))

    placed = (P(None, "gx", "gy", "gz"), P(None, "gx", "gy", "gz"), P(), P(), P(), P(), P())
    return jax.shard_map(
        on_device,
        mesh=mesh,
        in_specs=placed,
        out_specs=(P(None, "gx", "gy", "gz"), P(), P(), P(), P(), P()),
        check_vma=False,
    )
```

profile of v0, /device:TPU:1, one launch (start us, length us, event | category | flops | bytes accessed | tf_op | source)
XLA Modules:
  0.0 60.0 jit_solution(1888862397382019071)
XLA Ops:
  0.6 0.0 copy-start
  0.6 1.0 %copy-done = f32[16,8,8,128]{3,2,1,0:T(8,128)S(1)} copy-done((f32[16,8,8,128]{3,2,1,0:T(8,128)S(1)}, f32[16,8,8,128]{3,2,1,0:T(8,128)}, u32[]{:S(2)}) %copy-start) | copy-done | bytes 524312
  1.7 0.0 copy-start.1
  1.7 0.9 %copy-done.1 = f32[376,128]{1,0:T(8,128)S(1)} copy-done((f32[376,128]{1,0:T(8,128)S(1)}, f32[376,128]{1,0:T(8,128)}, u32[]{:S(2)}) %copy-start.1) | copy-done | bytes 192536
  2.6 0.0 copy-start.3
  2.6 0.7 %copy-done.3 = f32[16,16]{1,0:T(8,128)S(1)} copy-done((f32[16,16]{1,0:T(8,128)S(1)}, f32[16,16]{1,0:T(8,128)}, u32[]{:S(2)}) %copy-start.3) | copy-done | bytes 1048
  3.3 0.0 copy-start.4
  3.3 0.7 %copy-done.4 = f32[16,32]{1,0:T(8,128)S(1)} copy-done((f32[16,32]{1,0:T(8,128)S(1)}, f32[16,32]{1,0:T(8,128)}, u32[]{:S(2)}) %copy-start.4) | copy-done | bytes 2072
  4.0 0.0 copy-start.5
  4.0 0.8 %copy-done.5 = f32[16,2,2,32]{3,2,1,0:T(2,128)S(1)} copy-done((f32[16,2,2,32]{3,2,1,0:T(2,128)S(1)}, f32[16,2,2,32]{3,2,1,0:T(2,128)}, u32[]{:S(2)}) %copy-start.5) | copy-done | bytes 8216
  4.8 0.0 copy-start.6
  4.8 0.7 %copy-done.6 = f32[16,35]{1,0:T(8,128)S(1)} copy-done((f32[16,35]{1,0:T(8,128)S(1)}, f32[16,35]{1,0:T(8,128)}, u32[]{:S(2)}) %copy-start.6) | copy-done | bytes 2264
  5.5 0.0 copy-start.7
  5.5 0.7 %copy-done.7 = f32[16,16]{1,0:T(8,128)S(1)} copy-done((f32[16,16]{1,0:T(8,128)S(1)}, f32[16,16]{1,0:T(8,128)}, u32[]{:S(2)}) %copy-start.7) | copy-done | bytes 1048
  6.1 0.0 copy-start.8
  6.2 0.7 %copy-done.8 = f32[3,16]{1,0:T(4,128)S(1)} copy-done((f32[3,16]{1,0:T(4,128)S(1)}, f32[3,16]{1,0:T(4,128)}, u32[]{:S(2)}) %copy-start.8) | copy-done | bytes 216
  6.8 50.8 %shard_map.127.packed = f32[48,128]{1,0:T(8,128)S(1)} custom-call(f32[16,2,2,32]{3,2,1,0:T(2,128)S(1)} %copy-done.5, f32[16,8,8,128]{3,2,1,0:T(8,128)S(1)} %copy-done, f32[16,35]{1,0:T(8,128)S(1)} %copy-done.6, f32[16,16]{1,0:T(8,128)S(1)} %copy-done.3, f32[16,32]{1,0:T(8,128)S(1)} %copy-done.4, f32[16,16]{1,0:T(8,128)S(1)} %copy-done.7, ...), custom_call_target="tpu_custom_call" | custom-call | tf_op jit(solution)/shard_map/pallas_call | solution.py:800
  57.6 0.0 copy-start.2
  57.6 0.6 copy-done.2
  58.2 1.8 %shard_map.128 = (f32[16,2,2,32]{3,2,1,0:T(2,128)}, f32[16,35]{1,0:T(8,128)}, f32[16,16]{1,0:T(8,128)}, f32[16,32]{1,0:T(8,128)}, f32[16,16]{1,0:T(8,128)}, /*index=5*/f32[3,16]{1,0:T(4,128)}) custom-call(f32[48,128]{1,0:T(8,128)} %copy-done.2, f32[16,16]{1,0:T(8,128)} %edge_out.3, f32[16,32]{1,0:T(8,128)} %node_in.3, f32[3,16]{1,0:T(4,128)} %biases.3), custom_call_target="tpu_custom_call" | custom-call | tf_op jit(solution)/shard_map/pallas_call | solution.py:803
Async XLA Ops:
  0.6 1.0 %copy-start = (f32[16,8,8,128]{3,2,1,0:T(8,128)S(1)}, f32[16,8,8,128]{3,2,1,0:T(8,128)}, u32[]{:S(2)}) copy-start(f32[16,8,8,128]{3,2,1,0:T(8,128)} %cot_hbm.1) | copy-start | bytes 1572868
  1.7 0.9 %copy-start.1 = (f32[376,128]{1,0:T(8,128)S(1)}, f32[376,128]{1,0:T(8,128)}, u32[]{:S(2)}) copy-start(f32[376,128]{1,0:T(8,128)} %constant.2.clone.table) | copy-start | bytes 577540
  2.6 0.7 %copy-start.3 = (f32[16,16]{1,0:T(8,128)S(1)}, f32[16,16]{1,0:T(8,128)}, u32[]{:S(2)}) copy-start(f32[16,16]{1,0:T(8,128)} %edge_out.3) | copy-start | bytes 3076
  3.3 0.7 %copy-start.4 = (f32[16,32]{1,0:T(8,128)S(1)}, f32[16,32]{1,0:T(8,128)}, u32[]{:S(2)}) copy-start(f32[16,32]{1,0:T(8,128)} %node_in.3) | copy-start | bytes 6148
  4.0 0.8 %copy-start.5 = (f32[16,2,2,32]{3,2,1,0:T(2,128)S(1)}, f32[16,2,2,32]{3,2,1,0:T(2,128)}, u32[]{:S(2)}) copy-start(f32[16,2,2,32]{3,2,1,0:T(2,128)} %coarse.1) | copy-start | bytes 24580
  4.8 0.7 %copy-start.6 = (f32[16,35]{1,0:T(8,128)S(1)}, f32[16,35]{1,0:T(8,128)}, u32[]{:S(2)}) copy-start(f32[16,35]{1,0:T(8,128)} %edge_in.1) | copy-start | bytes 6724
  5.5 0.7 %copy-start.7 = (f32[16,16]{1,0:T(8,128)S(1)}, f32[16,16]{1,0:T(8,128)}, u32[]{:S(2)}) copy-start(f32[16,16]{1,0:T(8,128)} %node_out.1) | copy-start | bytes 3076
  6.1 0.7 %copy-start.8 = (f32[3,16]{1,0:T(4,128)S(1)}, f32[3,16]{1,0:T(4,128)}, u32[]{:S(2)}) copy-start(f32[3,16]{1,0:T(4,128)} %biases.3) | copy-start | bytes 580
  57.6 0.6 %copy-start.2 = (f32[48,128]{1,0:T(8,128)}, f32[48,128]{1,0:T(8,128)S(1)}, u32[]{:S(2)}) copy-start(f32[48,128]{1,0:T(8,128)S(1)} %shard_map.127.packed) | copy-start | bytes 73732
where the time goes:
time: 60.5 us; the launch traced here: 60 us
  Pallas kernels  52.6 us (87%)
  local copies, waits for them, and re-layouts  6.78 us (11%)
  between operations  0.66 us (1%)
    pallas_call x1, Pallas kernels, on_device(): make_main(sizes)  50.8 us
    unnamed x18, local copies, waits for them, and re-layouts  6.78 us
    pallas_call x1, Pallas kernels, on_device(): make_finish(float(nodes) ** (-0.5))(packed, edge_out, node_in, biases)  1.79 us

commit v1 on v0

--- a/solution.py
+++ b/solution.py
@@ -143,20 +143,20 @@
     n_plane = n_cols * n_z
 
     def kernel(
-        coarse, cot_hbm, edge_in, edge_out, node_in, node_out, biases, table,
+        coarse_in, cot_in, edge_in_in, edge_out_in, node_in_in, node_out_in, biases_in, table_in,
         out,
-        cot, p0, zr, tb, xr, vx, yr, means, lhs_rows, rows, e_all, e_sum, s_all, hn_all, u_all, g_all, xf,
+        coarse, cot, edge_in, edge_out, node_in, node_out, biases, table, p0, zr, tb, xr, vx, yr, means, lhs_rows, rows, e_all, e_sum, s_all, hn_all, u_all, g_all, xf,
         gm, yb, gy_all, xb, gx_all, zb, payload, core_slot, col_slots, plane_slots, total,
-        cot_sem, zf_s, zf_r, xf_s, xf_r, yf_s, yf_r, yb_s, yb_r, xb_s, xb_r, zb_s, zb_r,
+        load_sem, zf_s, zf_r, xf_s, xf_r, yf_s, yf_r, yb_s, yb_r, xb_s, xb_r, zb_s, zb_r,
         core_s, core_r, col_s, col_r, plane_s, plane_r, cast_s, cast_r,
     ):
         ix, iy, iz = lax.axis_index("gx"), lax.axis_index("gy"), lax.axis_index("gz")
         low = lax.rem(ix, Z_LOW)
         core = lax.rem(iy, CORES)
         layer = (iy // CORES) * Z_LOW + low
-        on_core0 = core == 0
-        is_root = on_core0 & (layer == 0)
-        is_leaf = on_core0 & (layer != 0)
+        on_core1 = core == 1
+        is_root = on_core1 & (layer == 0)
+        is_leaf = on_core1 & (layer != 0)
 
         def at_x(d):
             return (lax.rem(ix + (d + n_x), n_x), iy, iz)
@@ -168,7 +168,7 @@
             return (ix, iy, lax.rem(iz + (d + n_z), n_z))
 
         sibling = (ix, iy + 1 - 2 * core, iz)
-        column_root = (ix - low, 0, iz)
+        column_root = (ix - low, 1, iz)
 
         def in_column(k, c):
             return (ix + k % Z_LOW, (k // Z_LOW) * CORES + c, iz)
@@ -185,8 +185,22 @@
         def signal(device):
             pl.semaphore_signal(barrier, inc=1, device_id=device, device_id_type=MESH)
 
-        load_cot = pltpu.make_async_copy(cot_hbm, cot, cot_sem)
-        load_cot.start()
+        loads = [
+            pltpu.make_async_copy(src, dst, load_sem.at[i])
+            for i, (src, dst) in enumerate(
+                (
+                    (coarse_in, coarse),
+                    (edge_in_in, edge_in),
+                    (edge_out_in, edge_out),
+                    (node_in_in, node_in),
+                    (node_out_in, node_out),
+                    (biases_in, biases),
+                    (table_in, table),
+                    (cot_in, cot),
+                )
+            )
+        ]
+        loads[0].start()
         barrier = pltpu.get_barrier_semaphore()
         for d in (-1, 1):
             signal(at_z(d))
@@ -195,19 +209,18 @@
         for d in STEPS:
             signal(at_y(d))
 
-        @pl.when(layer != 0)
-        def _():
-            signal(column_root)
-
         @pl.when(is_root)
         def _():
             for k in range(1, n_layers):
-                signal(in_column(k, 0))
+                signal(in_column(k, 1))
             for k in range(1, n_plane):
                 signal(in_plane(k))
 
-        expected = 10 + jnp.where(is_leaf, 1, 0) + jnp.where(is_root, CORES * (n_layers - 1) + n_plane - 1, 0)
-
+        for c in loads[1:]:
+            c.start()
+        expected = 10 + jnp.where(is_leaf, 1, 0) + jnp.where(is_root, n_plane - 1, 0)
+
+        loads[0].wait()
         block = coarse[...]
         p0[...] = jnp.concatenate([block[:, p, q, :] for q in (0, 1) for p in (0, 1)], axis=1)
         pl.semaphore_wait(barrier, expected)
@@ -219,6 +232,8 @@
         for c in z_sends:
             c.start()
 
+        for c in loads[1:7]:
+            c.wait()
         w_own, w_other = edge_in[:, 0:16], edge_in[:, 16:32]
         col_x, col_y, col_z = edge_in[:, 32:33], edge_in[:, 33:34], edge_in[:, 34:35]
         n_own, n_gathered = node_in[:, 0:16], node_in[:, 16:32]
@@ -276,7 +291,7 @@
         for c in x_sends:
             c.start()
 
-        load_cot.wait()
+        loads[7].wait()
         for k in range(4):
             wide = jnp.concatenate([cot[:, 2 * k + i].reshape(128, 128) for i in (0, 1)], axis=1)
             u_all[:, :, 256 * k : 256 * k + 256] = mm(out_back, split(wide)).reshape(16, 8, 256)
@@ -521,6 +536,58 @@
             both = jnp.where(low_half, nxt[r_up, :] + pltpu.roll(nxt[r_down, :], 64, 1), 0.0)
             others[q] = both + fields[q][2] if q in (0, 1) else both
 
+        summed_out = jnp.where(same_y, outer_out, 0.0)
+        summed_in = jnp.where(same_y, outer_in, 0.0)
+        big = exact_mm(delta, split(jnp.concatenate([summed_out, summed_in], axis=1)))
+        r2, c2 = iota((128, 256), 0), iota((128, 256), 1)
+        placing = ones_where((c2 // 128 * 16 + c2 % 128 // 8) == r2).astype(BF16)
+        part = mm_exact(split(big), placing, NT)
+        r8, l8 = iota((8, 128), 0), iota((8, 128), 1)
+
+        def marked(r, mask):
+            return ones_where((r8 == r) & mask)
+
+        def right(first, rows16, special):
+            pieces = []
+            if rows16 is None:
+                pieces.append(jnp.zeros((80, 128), F32))
+            else:
+                if first > 0:
+                    pieces.append(jnp.zeros((first, 128), F32))
+                pieces.append(rows16)
+                if first < 64:
+                    pieces.append(jnp.zeros((64 - first, 128), F32))
+            pieces += [special, jnp.zeros((40, 128), F32)]
+            return jnp.concatenate(pieces, axis=0)
+
+        lefts, rights = [], []
+        none8 = jnp.zeros((8, 128), F32)
+        for q in (-1, 0, 1, 2):
+            m = means[q + 1]
+            if q in (0, 1):
+                lefts.append(fields[q][0])
+                rights.append(right(32, jnp.where(low_half, 0.0, pltpu.roll(m, 64, 1)), marked(4, l8 >= 64)))
+                lefts.append(fields[q][1])
+                rights.append(right(48, m * low_lanes, marked(3, l8 < 64) + marked(0, (l8 >= 64) & (l8 < 96))))
+            lefts.append(others[q])
+            rights.append(right(64, m, marked(2, (l8 % 32 == 20) & (l8 < 64)) if q in (0, 1) else none8))
+        lefts += [std[32:48, 0:128], nxt[128:144, :], nxt[144:160, :]]
+        rights += [
+            right(0, None, marked(5, l8 >= 64)),
+            right(0, None, marked(1, l8 < 64)),
+            right(0, None, marked(1, l8 >= 64)),
+        ]
+        payload[...] = part + mm(split(jnp.concatenate(lefts, axis=1)), split(jnp.concatenate(rights, axis=1)), NT)
+
+        to_second = send(payload, core_slot, core_s, core_r, sibling)
+        to_first = send(total, total, cast_s.at[0], cast_r, sibling)
+        slot = jnp.maximum(layer - 1, 0)
+        to_root = send(payload, col_slots.at[slot], col_s, col_r.at[slot], column_root)
+
+        @pl.when(core == 0)
+        def _():
+            to_second.start()
+
         zero = jnp.zeros((16, 128), F32)
         stacked = []
         for q in (-1, 0, 1, 2):
@@ -547,59 +614,9 @@
         for c in y_back:
             c.start()
 
-        summed_out = jnp.where(same_y, outer_out, 0.0)
-        summed_in = jnp.where(same_y, outer_in, 0.0)
-        big = exact_mm(delta, split(jnp.concatenate([summed_out, summed_in], axis=1)))
-        r2, c2 = iota((128, 256), 0), iota((128, 256), 1)
-        placing = ones_where((c2 // 128 * 16 + c2 % 128 // 8) == r2).astype(BF16)
-        part = mm_exact(split(big), placing, NT)
-        r8, l8 = iota((8, 128), 0), iota((8, 128), 1)
-
-        def marked(r, mask):
-            return ones_where((r8 == r) & mask)
-
-        def right(first, rows16, special):
-            pieces = []
-            if rows16 is None:
-                pieces.append(jnp.zeros((80, 128), F32))
-            else:
-                if first > 0:
-                    pieces.append(jnp.zeros((first, 128), F32))
-                pieces.append(rows16)
-                if first < 64:
-                    pieces.append(jnp.zeros((64 - first, 128), F32))
-            pieces += [special, jnp.zeros((40, 128), F32)]
-            return jnp.concatenate(pieces, axis=0)
-
-        lefts, rights = [], []
-        none8 = jnp.zeros((8, 128), F32)
-        for q in (-1, 0, 1, 2):
-            m = means[q + 1]
-            if q in (0, 1):
-                lefts.append(fields[q][0])
-                rights.append(right(32, jnp.where(low_half, 0.0, pltpu.roll(m, 64, 1)), marked(4, l8 >= 64)))
-                lefts.append(fields[q][1])
-                rights.append(right(48, m * low_lanes, marked(3, l8 < 64) + marked(0, (l8 >= 64) & (l8 < 96))))
-            lefts.append(others[q])
-            rights.append(right(64, m, marked(2, (l8 % 32 == 20) & (l8 < 64)) if q in (0, 1) else none8))
-        lefts += [std[32:48, 0:128], nxt[128:144, :], nxt[144:160, :]]
-        rights += [
-            right(0, None, marked(5, l8 >= 64)),
-            right(0, None, marked(1, l8 < 64)),
-            right(0, None, marked(1, l8 >= 64)),
-        ]
-        payload[...] = part + mm(split(jnp.concatenate(lefts, axis=1)), split(jnp.concatenate(rights, axis=1)), NT)
-
-        to_core0 = send(payload, core_slot, core_s, core_r, sibling)
-        to_root = send(payload, col_slots.at[jnp.maximum(layer - 1, 0)], col_s, col_r.at[jnp.maximum(layer - 1, 0)], column_root)
-
-        @pl.when(core == 1)
-        def _():
-            to_core0.start()
-
-        @pl.when(on_core0)
-        def _():
-            to_core0.wait_recv()
+        @pl.when(on_core1)
+        def _():
+            to_second.wait_recv()
             payload[...] = payload[...] + core_slot[...]
 
         @pl.when(is_leaf)
@@ -631,7 +648,7 @@
         def _():
             value = payload[...]
             for k in range(n_layers - 1):
-                send(payload, col_slots.at[k], col_s, col_r.at[k], in_column(k + 1, 0)).wait_recv()
+                send(payload, col_slots.at[k], col_s, col_r.at[k], in_column(k + 1, 1)).wait_recv()
                 value = value + col_slots[k]
             plane_slots[my_place] = value
             for c in to_plane:
@@ -655,12 +672,7 @@
         for c in z_back:
             c.start()
 
-        to_all = [
-            send(total, total, cast_s.at[CORES * k + c], cast_r, in_column(k, c))
-            for k in range(n_layers)
-            for c in range(CORES)
-            if (k, c) != (0, 0)
-        ]
+        up_column = [send(total, total, cast_s.at[k], cast_r, in_column(k, 1)) for k in range(1, n_layers)]
 
         @pl.when(is_root)
         def _():
@@ -670,7 +682,7 @@
             for k in range(1, n_plane):
                 value = value + plane_slots[k]
             total[...] = value
-            for c in to_all:
+            for c in [to_first] + up_column:
                 c.start()
 
         for c in z_back:
@@ -686,16 +698,27 @@
 
         @pl.when(jnp.logical_not(is_root))
         def _():
-            to_all[0].wait_recv()
+            to_first.wait_recv()
+
+        @pl.when(is_leaf)
+        def _():
+            to_first.start()
 
         out[32:48, :] = total[...]
+        out[48:64, 0:32] = node_in[...]
+        out[48:64, 32:48] = edge_out[...]
+        out[64:67, 0:16] = biases[...]
 
         for c in z_sends + x_sends + y_sends + y_back + x_back + z_back:
             c.wait_send()
 
-        @pl.when(core == 1)
-        def _():
-            to_core0.wait_send()
+        @pl.when(core == 0)
+        def _():
+            to_second.wait_send()
+
+        @pl.when(on_core1)
+        def _():
+            to_first.wait_send()
 
         @pl.when(is_leaf)
         def _():
@@ -703,7 +726,7 @@
 
         @pl.when(is_root)
         def _():
-            for c in to_plane + to_all:
+            for c in to_plane + up_column:
                 c.wait_send()
 
     block = pltpu.VMEM((16, 128), F32)
@@ -713,7 +736,14 @@
 
     dma = pltpu.SemaphoreType.DMA
     scratch = [
+        pltpu.VMEM((16, 2, 2, 32), F32),
         pltpu.VMEM((16, 8, 8, 128), F32),
+        pltpu.VMEM((16, 35), F32),
+        pltpu.VMEM((16, 16), F32),
+        pltpu.VMEM((16, 32), F32),
+        pltpu.VMEM((16, 16), F32),
+        pltpu.VMEM((3, 16), F32),
+        pltpu.VMEM((TABLE_ROWS, 128), F32),
         block,
         blocks(2),
         block,
@@ -741,53 +771,66 @@
         blocks(n_layers - 1),
         blocks(n_plane),
         block,
-        dma,
+        dma((8,)),
         dma((2,)), dma((2,)), dma((4,)), dma((4,)), dma((4,)), dma((4,)),
         dma((4,)), dma((4,)), dma((4,)), dma((4,)), dma((2,)), dma((2,)),
-        dma, dma, dma, dma((n_layers - 1,)), dma((n_plane,)), dma((n_plane,)), dma((CORES * n_layers,)), dma,
+        dma, dma, dma, dma((n_layers - 1,)), dma((n_plane,)), dma((n_plane,)), dma((n_layers,)), dma,
     ]
     vmem = pl.BlockSpec(memory_space=pltpu.VMEM)
     return pl.pallas_call(
         kernel,
-        out_shape=jax.ShapeDtypeStruct((48, 128), F32),
-        in_specs=[vmem, pl.BlockSpec(memory_space=pl.ANY)] + [vmem] * 6,
+        out_shape=jax.ShapeDtypeStruct((72, 128), F32),
+        in_specs=[pl.BlockSpec(memory_space=pltpu.HBM)] * 8,
         out_specs=vmem,
         scratch_shapes=scratch,
         compiler_params=pltpu.CompilerParams(
-            collective_id=0, has_side_effects=True, vmem_limit_bytes=40 * 1024 * 1024
+            collective_id=0, has_side_effects=True, vmem_limit_bytes=60 * 1024 * 1024
         ),
     )
 
 
 def make_finish(factor):
-    def kernel(packed, edge_out, node_in, biases, grad_coarse, g_edge_in, g_edge_out, g_node_in, g_node_out, g_biases):
+    shapes = ((16, 2, 2, 32), (16, 35), (16, 16), (16, 32), (16, 16), (3, 16))
+
+    def kernel(packed, *refs):
+        outs, buffers, sem = refs[:6], refs[6:12], refs[12]
+        grad_coarse, g_edge_in, g_edge_out, g_node_in, g_node_out, g_biases = buffers
+        copies = [pltpu.make_async_copy(src, dst, sem.at[i]) for i, (src, dst) in enumerate(zip(buffers, outs))]
         for q in (0, 1):
             block = packed[16 * q : 16 * q + 16, :]
             for p in (0, 1):
                 grad_coarse[:, p, q, :] = block[:, 32 * p : 32 * p + 32]
+        copies[0].start()
         total = packed[32:48, :] * factor
         g_node_out[...] = total[:, 0:16]
+        copies[4].start()
         g_edge_in[...] = total[:, 48:83]
-        n_gathered = node_in[:, 16:32]
+        copies[1].start()
+        n_gathered, edge_out, b1_row = packed[48:64, 16:32], packed[48:64, 32:48], packed[65:66, 0:16]
         eye = ones_where(iota((16, 16), 0) == iota((16, 16), 1)).astype(BF16)
         n_back = exact_mm(eye, split(n_gathered), NT)
         back = mm(split(n_back), split(total))
         g_edge_out[...] = back[:, 16:32]
+        copies[2].start()
         outer_in = total[:, 16:32]
         g_node_in[:, 0:16] = total[:, 32:48]
-        g_node_in[:, 16:32] = mm(split(outer_in), split(edge_out[...]), NT) + total[:, 85:86] * biases[1:2, :]
+        g_node_in[:, 16:32] = mm(split(outer_in), split(edge_out), NT) + total[:, 85:86] * b1_row
+        copies[3].start()
         rows = jnp.concatenate([total, back], axis=1)
         r, c = iota((8, 256), 0), iota((8, 256), 1)
         pick = ones_where(((r == 0) & (c == 83)) | ((r == 1) & (c == 128 + 85)) | ((r == 2) & (c == 84))).astype(BF16)
         g_biases[...] = exact_mm(pick, split(rows), NT)[0:3, :]
-
-    vmem = pl.BlockSpec(memory_space=pltpu.VMEM)
-    shapes = ((16, 2, 2, 32), (16, 35), (16, 16), (16, 32), (16, 16), (3, 16))
+        copies[5].start()
+        for c in copies:
+            c.wait()
+
     return pl.pallas_call(
         kernel,
         out_shape=[jax.ShapeDtypeStruct(s, F32) for s in shapes],
-        in_specs=[vmem] * 4,
-        out_specs=[vmem] * 6,
+        in_specs=[pl.BlockSpec(memory_space=pltpu.VMEM)],
+        out_specs=[pl.BlockSpec(memory_space=pltpu.HBM)] * 6,
+        scratch_shapes=[pltpu.VMEM(s, F32) for s in shapes] + [pltpu.SemaphoreType.DMA((6,))],
+        compiler_params=pltpu.CompilerParams(vmem_limit_bytes=4 * 1024 * 1024),
     )
 
 
@@ -800,7 +843,7 @@
         packed = make_main(sizes)(
             coarse, cotangent, edge_in, edge_out, node_in, node_out, biases, jnp.asarray(table)
         )
-        return tuple(make_finish(float(nodes) ** -0.5)(packed, edge_out, node_in, biases))
+        return tuple(make_finish(float(nodes) ** -0.5)(packed))
 
     placed = (P(None, "gx", "gy", "gz"), P(None, "gx", "gy", "gz"), P(), P(), P(), P(), P())
     return jax.shard_map(

time: 60.5 us -> 51.5 us (0.85)
  local copies, waits for them, and re-layouts: 6.78 us -> 0.76 us
  Pallas kernels: 52.6 us -> 49.7 us
    unnamed x18 -> x2, local copies, waits for them, and re-layouts: 6.78 us -> 0.76 us
    pallas_call x1, Pallas kernels: 50.8 us -> 48.7 us  [on_device(): make_main(sizes)]
    pallas_call x1, Pallas kernels: 1.79 us -> 1.06 us  [on_device(): return tuple(make_finish(float(nodes) ** (-0.5))(packed))]
where the time goes in v1:
time: 51.5 us; the launch traced here: 51.2 us
  Pallas kernels  49.7 us (97%)
  local copies, waits for them, and re-layouts  0.76 us (1%)
  between operations  0.65 us (1%)
    pallas_call x1, Pallas kernels, on_device(): make_main(sizes)  48.7 us
    pallas_call x1, Pallas kernels, on_device(): return tuple(make_finish(float(nodes) ** (-0.5))(packed))  1.06 us

profile of v1, /device:TPU:1, one launch (start us, length us, event | category | flops | bytes accessed | tf_op | source)
XLA Modules:
  0.0 51.2 jit_solution(18120551971947833721)
XLA Ops:
  0.6 48.7 %shard_map.127.packed = f32[72,128]{1,0:T(8,128)} custom-call(f32[16,2,2,32]{3,2,1,0:T(2,128)} %coarse_in.1, f32[16,8,8,128]{3,2,1,0:T(8,128)} %cot_in.1, f32[16,35]{1,0:T(8,128)} %edge_in_in.1, f32[16,16]{1,0:T(8,128)} %edge_out_in.1, f32[16,32]{1,0:T(8,128)} %node_in_in.1, f32[16,16]{1,0:T(8,128)} %node_out_in.1, f32[3,16]{1,0:T(4,128)} %biases_in.1, ...), custom_call_target="tpu_custom_call" | custom-call | tf_op jit(solution)/shard_map/pallas_call | solution.py:843
  49.3 0.0 copy-start
  49.3 0.8 %copy-done = f32[72,128]{1,0:T(8,128)S(1)} copy-done((f32[72,128]{1,0:T(8,128)S(1)}, f32[72,128]{1,0:T(8,128)}, u32[]{:S(2)}) %copy-start) | copy-done | bytes 36888
  50.1 1.1 %shard_map.128 = (f32[16,2,2,32]{3,2,1,0:T(2,128)}, f32[16,35]{1,0:T(8,128)}, f32[16,16]{1,0:T(8,128)}, f32[16,32]{1,0:T(8,128)}, f32[16,16]{1,0:T(8,128)}, /*index=5*/f32[3,16]{1,0:T(4,128)}) custom-call(f32[72,128]{1,0:T(8,128)S(1)} %copy-done), custom_call_target="tpu_custom_call" | custom-call | tf_op jit(solution)/shard_map/pallas_call | solution.py:846
Async XLA Ops:
  49.3 0.8 %copy-start = (f32[72,128]{1,0:T(8,128)S(1)}, f32[72,128]{1,0:T(8,128)}, u32[]{:S(2)}) copy-start(f32[72,128]{1,0:T(8,128)} %shard_map.127.packed) | copy-start | bytes 110596

commit v2 on v1

--- a/solution.py
+++ b/solution.py
@@ -31,9 +31,14 @@
 ABSENT = -1.0e5
 SLOT = {0: 0, 1: 1, -1: 2, 2: 3}
 STEPS = (-2, -1, 1, 2)
+WIDE = (-2, -1, 0, 1, 2)
+XZ = tuple((x, z) for x in WIDE for z in (-1, 0, 1) if (x, z) != (0, 0))
+ROUND = tuple(d for d in XZ if d[1] != 0)
+LEVEL = tuple(d for d in XZ if d[1] == 0)
 
 RZ, RZ_UP, RZ_DOWN, PROFILES, Y_STD, Y_NEXT, Y_GAP, DELTA = 0, 32, 64, 96, 136, 168, 296, 328
-TABLE_ROWS = 376
+ALONG_Z = 376
+TABLE_ROWS = 504
 
 
 def make_table():
@@ -82,6 +87,7 @@
             table[DELTA + c, lane] = 1.0
             table[DELTA + 16 + c, lane] = 1.0 if y == 0 else 0.0
             table[DELTA + 32 + c, lane] = 1.0 if y == 7 else 0.0
+    table[ALONG_Z : ALONG_Z + 128, 0:96] = table[RZ : RZ + 96].T
     return table.astype(np.float32)
 
 
@@ -100,11 +106,12 @@
 
 def mm(a, b, dims=NN):
     (ah, al), (bh, bl) = a, b
-    return dot(ah, bh, dims) + (dot(ah, bl, dims) + dot(al, bh, dims))
+    at = dims[0][1][0]
+    return dot(jnp.concatenate([ah, ah, al], axis=1), jnp.concatenate([bh, bl, bh], axis=at), dims)
 
 
 def mm_exact(a, b, dims=NN):
-    return dot(a[0], b, dims) + dot(a[1], b, dims)
+    return dot(jnp.concatenate([a[0], a[1]], axis=1), jnp.concatenate([b, b], axis=dims[0][1][0]), dims)
 
 
 def exact_mm(a, b, dims=NN):
@@ -145,9 +152,9 @@
     def kernel(
         coarse_in, cot_in, edge_in_in, edge_out_in, node_in_in, node_out_in, biases_in, table_in,
         out,
-        coarse, cot, edge_in, edge_out, node_in, node_out, biases, table, p0, zr, tb, xr, vx, yr, means, lhs_rows, rows, e_all, e_sum, s_all, hn_all, u_all, g_all, xf,
-        gm, yb, gy_all, xb, gx_all, zb, payload, core_slot, col_slots, plane_slots, total,
-        load_sem, zf_s, zf_r, xf_s, xf_r, yf_s, yf_r, yb_s, yb_r, xb_s, xb_r, zb_s, zb_r,
+        coarse, cot, edge_in, edge_out, node_in, node_out, biases, table, p0, p0_rim, xr, rim_r, vx, yr, means, lhs_rows, rows, e_all, e_sum, s_all, hn_all, u_all, g_all, xf,
+        gm, yb, back_blocks, back_rims, xb, rim_b, payload, core_slot, col_slots, plane_slots, total,
+        load_sem, xf_s, xf_r, yf_s, yf_r, yb_s, yb_r, xb_s, xb_r,
         core_s, core_r, col_s, col_r, plane_s, plane_r, cast_s, cast_r,
     ):
         ix, iy, iz = lax.axis_index("gx"), lax.axis_index("gy"), lax.axis_index("gz")
@@ -158,14 +165,11 @@
         is_root = on_core1 & (layer == 0)
         is_leaf = on_core1 & (layer != 0)
 
-        def at_x(d):
-            return (lax.rem(ix + (d + n_x), n_x), iy, iz)
+        def at_xz(d):
+            return (lax.rem(ix + (d[0] + n_x), n_x), iy, lax.rem(iz + (d[1] + n_z), n_z))
 
         def at_y(d):
             return (ix, lax.rem(iy + (d + n_y), n_y), iz)
-
-        def at_z(d):
-            return (ix, iy, lax.rem(iz + (d + n_z), n_z))
 
         sibling = (ix, iy + 1 - 2 * core, iz)
         column_root = (ix - low, 1, iz)
@@ -202,10 +206,8 @@
         ]
         loads[0].start()
         barrier = pltpu.get_barrier_semaphore()
-        for d in (-1, 1):
-            signal(at_z(d))
-        for d in STEPS:
-            signal(at_x(d))
+        for d in XZ:
+            signal(at_xz(d))
         for d in STEPS:
             signal(at_y(d))
 
@@ -218,18 +220,39 @@
 
         for c in loads[1:]:
             c.start()
-        expected = 10 + jnp.where(is_leaf, 1, 0) + jnp.where(is_root, n_plane - 1, 0)
+        expected = len(XZ) + len(STEPS) + jnp.where(is_leaf, 1, 0) + jnp.where(is_root, n_plane - 1, 0)
+
+        lane = iota((16, 128), 1)
+        group, place = lane // 32, lane % 32
+        rim = (place[0:8] < 3) | (place[0:8] >= 29)
+
+        def pack_rims(block):
+            return jnp.where(rim, block[0:8, :], pltpu.roll(block[8:16, :], 120, 1))
+
+        def unpack_rims(block):
+            return jnp.concatenate([block, pltpu.roll(block, 8, 1)], axis=0)
 
         loads[0].wait()
         block = coarse[...]
-        p0[...] = jnp.concatenate([block[:, p, q, :] for q in (0, 1) for p in (0, 1)], axis=1)
+        block = jnp.concatenate([block[:, p, q, :] for q in (0, 1) for p in (0, 1)], axis=1)
+        p0[...] = block
+        p0_rim[...] = pack_rims(block)
         pl.semaphore_wait(barrier, expected)
 
-        z_sends = [
-            send(p0, zr.at[0], zf_s.at[0], zf_r.at[0], at_z(1)),
-            send(p0, zr.at[1], zf_s.at[1], zf_r.at[1], at_z(-1)),
-        ]
-        for c in z_sends:
+        def round_xz(level_src, level_dst, rim_src, rim_dst, send_sems, recv_sems):
+            copies = []
+            for d in ROUND + LEVEL:
+                back = (-d[0], -d[1])
+                i = XZ.index(back)
+                if d[1] == 0:
+                    src, dst = level_src(d[0]), level_dst.at[LEVEL.index(back)]
+                else:
+                    src, dst = rim_src(d[0]), rim_dst.at[ROUND.index(back)]
+                copies.append(send(src, dst, send_sems.at[i], recv_sems.at[i], at_xz(d)))
+            return copies
+
+        x_sends = round_xz(lambda d: p0, xr, lambda d: p0_rim, rim_r, xf_s, xf_r)
+        for c in x_sends:
             c.start()
 
         for c in loads[1:7]:
@@ -262,8 +285,6 @@
         b0_col, b1_row, b2_col = bias_cols[:, 0:1], bias_rows[1:2, :], bias_cols[:, 2:3]
         nb_col = jnp.sum(n_gathered * b1_row, axis=1, keepdims=True)
         maps = vertex_maps()
-        lane = iota((16, 128), 1)
-        group, place = lane // 32, lane % 32
         gap_lane = ones_where((place == 20) & (group < 2))
 
         def blocks4(first):
@@ -276,20 +297,13 @@
             )
 
         rz, rz_up, rz_down = blocks4(RZ), blocks4(RZ_UP), blocks4(RZ_DOWN)
-
-        z_sends[0].wait_recv()
-        z_sends[1].wait_recv()
-        tb[...] = (
-            mm_exact(split(p0[...]), maps[0])
-            + mm_exact(split(zr[0]), maps[1])
-            + mm_exact(split(zr[1]), maps[2])
-        )
-        x_sends = []
-        for d in STEPS:
-            i = STEPS.index(-d)
-            x_sends.append(send(tb, xr.at[i], xf_s.at[i], xf_r.at[i], at_x(d)))
-        for c in x_sends:
-            c.start()
+        back_z = table[ALONG_Z : ALONG_Z + 128, :]
+        group_z = iota((128, 128), 1) // 32
+
+        def back_blocks_z(kind, n):
+            return split(jnp.concatenate([jnp.where(group_z == i, spread(back_z, i - kind), 0.0) for i in range(n)], axis=0))
+
+        to_rz, to_rz_up, to_rz_down = back_blocks_z(0, 4), back_blocks_z(1, 2), back_blocks_z(2, 2)
 
         loads[7].wait()
         for k in range(4):
@@ -304,9 +318,13 @@
 
         for c in x_sends:
             c.wait_recv()
-        x_blocks = {0: tb[...]}
-        for i, d in enumerate(STEPS):
-            x_blocks[d] = xr[i]
+        pieces = []
+        for d in WIDE:
+            level = p0[...] if d == 0 else xr[LEVEL.index((d, 0))]
+            rims = [unpack_rims(rim_r[ROUND.index((d, z))]) for z in (-1, 1)]
+            pieces.append(jnp.concatenate([level] + rims, axis=1))
+        summed = mm_exact(split(jnp.concatenate(pieces, axis=0)), jnp.concatenate(maps, axis=0))
+        x_blocks = {d: summed[16 * i : 16 * i + 16, :] for i, d in enumerate(WIDE)}
         for q in (0, 1):
             acc = jnp.zeros((16, 128), F32)
             for vertex in (-1, 0, 1, 2):
@@ -507,14 +525,13 @@
         def along_z(first, n, by):
             return mm(
                 split(xf[:, :, 128 * first : 128 * (first + n)].reshape(128, 128 * n)),
-                (by[0][:, 0 : 128 * n], by[1][:, 0 : 128 * n]),
-                NT,
+                (by[0][0 : 128 * n, :], by[1][0 : 128 * n, :]),
             )
 
-        z1 = along_z(0, 4, rz)
-        z2 = along_z(4, 3, rz)
-        z3 = along_z(7, 4, rz) + along_z(15, 2, rz_up) + along_z(17, 2, rz_down)
-        z4 = along_z(11, 4, rz)
+        z1 = along_z(0, 4, to_rz)
+        z2 = along_z(4, 3, to_rz)
+        z3 = along_z(7, 4, to_rz) + along_z(15, 2, to_rz_up) + along_z(17, 2, to_rz_down)
+        z4 = along_z(11, 4, to_rz)
         counting = (
             6.0 * table[DELTA : DELTA + 16, :]
             - wall_low * table[DELTA + 16 : DELTA + 32, :]
@@ -623,18 +640,35 @@
         def _():
             to_root.start()
 
+        edge_place = (place[0:8] < 2) | (place[0:8] == 17) | (place[0:8] == 18)
+
+        def pack_back(block):
+            return jnp.where(edge_place, block[0:8, :], pltpu.roll(block[8:16, :], 8, 1))
+
+        def unpack_back(block):
+            return jnp.concatenate([block, pltpu.roll(block, 120, 1)], axis=0)
+
         for c in y_back:
             c.wait_recv()
+        own_rows = []
         for q in (0, 1):
             value = gm[q + 1]
             for d in (-2, -1, 1, 2):
                 if (d, q) not in ((-2, 1), (2, 0)):
                     value = value + yb[STEPS.index(d), q] * there[d]
-            gy_all[q] = value
-        x_back = []
-        for d in STEPS:
-            i = STEPS.index(-d)
-            x_back.append(send(gy_all, xb.at[i], xb_s.at[i], xb_r.at[i], at_x(d)))
+            own_rows.append(value)
+        for i, d in enumerate(WIDE):
+            value = jnp.zeros((16, 128), F32)
+            for q in (0, 1):
+                for p in (0, 1):
+                    if p + d in SLOT:
+                        moved = spread(own_rows[q], 2 * q + p - SLOT[p + d])
+                        value = value + jnp.where(group == 2 * q + p, moved, 0.0)
+            back_blocks[i] = value
+            back_rims[i] = pack_back(value)
+        x_back = round_xz(
+            lambda d: back_blocks.at[WIDE.index(d)], xb, lambda d: back_rims.at[WIDE.index(d)], rim_b, xb_s, xb_r
+        )
         for c in x_back:
             c.start()
 
@@ -653,24 +687,6 @@
             plane_slots[my_place] = value
             for c in to_plane:
                 c.start()
-
-        for c in x_back:
-            c.wait_recv()
-        for q in (0, 1):
-            value = gy_all[q]
-            for d in (-2, -1, 1, 2):
-                for p in (0, 1):
-                    vertex = p - d
-                    if vertex in SLOT:
-                        moved = spread(xb[STEPS.index(d), q], p - SLOT[vertex])
-                        value = value + jnp.where(group == p, moved, 0.0)
-            gx_all[q] = jnp.where(low_half, value, 0.0)
-        z_back = [
-            send(gx_all, zb.at[0], zb_s.at[0], zb_r.at[0], at_z(1)),
-            send(gx_all, zb.at[1], zb_s.at[1], zb_r.at[1], at_z(-1)),
-        ]
-        for c in z_back:
-            c.start()
 
         up_column = [send(total, total, cast_s.at[k], cast_r, in_column(k, 1)) for k in range(1, n_layers)]
 
@@ -685,16 +701,20 @@
             for c in [to_first] + up_column:
                 c.start()
 
-        for c in z_back:
+        for c in x_back:
             c.wait_recv()
-        for q in (0, 1):
-            value = (
-                mm_exact(split(gx_all[q]), maps[0], NT)
-                + mm_exact(split(zb[0, q]), maps[2], NT)
-                + mm_exact(split(zb[1, q]), maps[1], NT)
-            )
-            neighbour = there[-1] if q == 0 else there[1]
-            out[16 * q : 16 * q + 16, :] = value * (0.25 / (1.0 + neighbour))
+        level = back_blocks[WIDE.index(0)]
+        for i in range(len(LEVEL)):
+            level = level + xb[i]
+        sides = []
+        for z in (-1, 1):
+            value = rim_b[ROUND.index((-2, z))]
+            for d in WIDE[1:]:
+                value = value + rim_b[ROUND.index((d, z))]
+            sides.append(unpack_back(value))
+        level, sides = split(level), [split(v) for v in sides]
+        value = mm_exact(level, maps[0], NT) + mm_exact(sides[0], maps[2], NT) + mm_exact(sides[1], maps[1], NT)
+        out[0:16, :] = value * jnp.where(group < 2, 0.25 / (1.0 + there[-1]), 0.25 / (1.0 + there[1]))
 
         @pl.when(jnp.logical_not(is_root))
         def _():
@@ -704,12 +724,12 @@
         def _():
             to_first.start()
 
-        out[32:48, :] = total[...]
-        out[48:64, 0:32] = node_in[...]
-        out[48:64, 32:48] = edge_out[...]
-        out[64:67, 0:16] = biases[...]
-
-        for c in z_sends + x_sends + y_sends + y_back + x_back + z_back:
+        out[16:32, :] = total[...]
+        out[32:48, 0:32] = node_in[...]
+        out[32:48, 32:48] = edge_out[...]
+        out[48:51, 0:16] = biases[...]
+
+        for c in x_sends + y_sends + y_back + x_back:
             c.wait_send()
 
         @pl.when(core == 0)
@@ -745,9 +765,9 @@
         pltpu.VMEM((3, 16), F32),
         pltpu.VMEM((TABLE_ROWS, 128), F32),
         block,
-        blocks(2),
-        block,
-        blocks(4),
+        pltpu.VMEM((8, 128), F32),
+        blocks(len(LEVEL)),
+        pltpu.VMEM((len(ROUND), 8, 128), F32),
         blocks(2),
         blocks(4, 2),
         blocks(4),
@@ -762,24 +782,23 @@
         pltpu.VMEM((16, 8, 19 * 128), F32),
         blocks(4),
         blocks(4, 2),
-        blocks(2),
-        blocks(4, 2),
-        blocks(2),
-        blocks(2, 2),
+        blocks(len(WIDE)),
+        pltpu.VMEM((len(WIDE), 8, 128), F32),
+        blocks(len(LEVEL)),
+        pltpu.VMEM((len(ROUND), 8, 128), F32),
         block,
         block,
         blocks(n_layers - 1),
         blocks(n_plane),
         block,
         dma((8,)),
-        dma((2,)), dma((2,)), dma((4,)), dma((4,)), dma((4,)), dma((4,)),
-        dma((4,)), dma((4,)), dma((4,)), dma((4,)), dma((2,)), dma((2,)),
+        dma((len(XZ),)), dma((len(XZ),)), dma((4,)), dma((4,)), dma((4,)), dma((4,)), dma((len(XZ),)), dma((len(XZ),)),
         dma, dma, dma, dma((n_layers - 1,)), dma((n_plane,)), dma((n_plane,)), dma((n_layers,)), dma,
     ]
     vmem = pl.BlockSpec(memory_space=pltpu.VMEM)
     return pl.pallas_call(
         kernel,
-        out_shape=jax.ShapeDtypeStruct((72, 128), F32),
+        out_shape=jax.ShapeDtypeStruct((56, 128), F32),
         in_specs=[pl.BlockSpec(memory_space=pltpu.HBM)] * 8,
         out_specs=vmem,
         scratch_shapes=scratch,
@@ -796,17 +815,17 @@
         outs, buffers, sem = refs[:6], refs[6:12], refs[12]
         grad_coarse, g_edge_in, g_edge_out, g_node_in, g_node_out, g_biases = buffers
         copies = [pltpu.make_async_copy(src, dst, sem.at[i]) for i, (src, dst) in enumerate(zip(buffers, outs))]
+        block = packed[0:16, :]
         for q in (0, 1):
-            block = packed[16 * q : 16 * q + 16, :]
             for p in (0, 1):
-                grad_coarse[:, p, q, :] = block[:, 32 * p : 32 * p + 32]
+                grad_coarse[:, p, q, :] = block[:, 32 * (2 * q + p) : 32 * (2 * q + p) + 32]
         copies[0].start()
-        total = packed[32:48, :] * factor
+        total = packed[16:32, :] * factor
         g_node_out[...] = total[:, 0:16]
         copies[4].start()
         g_edge_in[...] = total[:, 48:83]
         copies[1].start()
-        n_gathered, edge_out, b1_row = packed[48:64, 16:32], packed[48:64, 32:48], packed[65:66, 0:16]
+        n_gathered, edge_out, b1_row = packed[32:48, 16:32], packed[32:48, 32:48], packed[49:50, 0:16]
         eye = ones_where(iota((16, 16), 0) == iota((16, 16), 1)).astype(BF16)
         n_back = exact_mm(eye, split(n_gathered), NT)
         back = mm(split(n_back), split(total))

time: 51.5 us -> 49.7 us (0.965)
  Pallas kernels: 49.7 us -> 48.1 us
    pallas_call x1, Pallas kernels: 48.7 us -> 47 us  [on_device(): make_main(sizes)]
where the time goes in v2:
time: 49.7 us; the launch traced here: 49.5 us
  Pallas kernels  48.1 us (97%)
  local copies, waits for them, and re-layouts  0.74 us (1%)
  between operations  0.65 us (1%)
    pallas_call x1, Pallas kernels, on_device(): make_main(sizes)  47 us
    pallas_call x1, Pallas kernels, on_device(): return tuple(make_finish(float(nodes) ** (-0.5))(packed))  1.12 us

profile of v2, /device:TPU:1, one launch (start us, length us, event | category | flops | bytes accessed | tf_op | source)
XLA Modules:
  0.0 49.5 jit_solution(16808094576076618434)
XLA Ops:
  0.6 47.0 %shard_map.127.packed = f32[56,128]{1,0:T(8,128)} custom-call(f32[16,2,2,32]{3,2,1,0:T(2,128)} %coarse_in.1, f32[16,8,8,128]{3,2,1,0:T(8,128)} %cot_in.1, f32[16,35]{1,0:T(8,128)} %edge_in_in.1, f32[16,16]{1,0:T(8,128)} %edge_out_in.1, f32[16,32]{1,0:T(8,128)} %node_in_in.1, f32[16,16]{1,0:T(8,128)} %node_out_in.1, f32[3,16]{1,0:T(4,128)} %biases_in.1, ...), custom_call_target="tpu_custom_call" | custom-call | tf_op jit(solution)/shard_map/pallas_call | solution.py:862
  47.6 0.0 copy-start
  47.6 0.7 %copy-done = f32[56,128]{1,0:T(8,128)S(1)} copy-done((f32[56,128]{1,0:T(8,128)S(1)}, f32[56,128]{1,0:T(8,128)}, u32[]{:S(2)}) %copy-start) | copy-done | bytes 28696
  48.3 1.1 %shard_map.128 = (f32[16,2,2,32]{3,2,1,0:T(2,128)}, f32[16,35]{1,0:T(8,128)}, f32[16,16]{1,0:T(8,128)}, f32[16,32]{1,0:T(8,128)}, f32[16,16]{1,0:T(8,128)}, /*index=5*/f32[3,16]{1,0:T(4,128)}) custom-call(f32[56,128]{1,0:T(8,128)S(1)} %copy-done), custom_call_target="tpu_custom_call" | custom-call | tf_op jit(solution)/shard_map/pallas_call | solution.py:865
Async XLA Ops:
  47.6 0.7 %copy-start = (f32[56,128]{1,0:T(8,128)S(1)}, f32[56,128]{1,0:T(8,128)}, u32[]{:S(2)}) copy-start(f32[56,128]{1,0:T(8,128)} %shard_map.127.packed) | copy-start | bytes 86020

commit v3 on v2

--- a/solution.py
+++ b/solution.py
@@ -91,6 +91,7 @@
     return table.astype(np.float32)
 
 
+RESULTS = ((16, 2, 2, 32), (16, 35), (16, 16), (16, 32), (16, 16), (3, 16))
 NN = (((1,), (0,)), ((), ()))
 NT = (((1,), (1,)), ((), ()))
 
@@ -142,7 +143,7 @@
     return maps
 
 
-def make_main(sizes):
+def make_main(sizes, factor):
     n_x, n_y, n_z = sizes
     z_high = n_y // CORES
     n_layers = z_high * Z_LOW
@@ -151,19 +152,24 @@
 
     def kernel(
         coarse_in, cot_in, edge_in_in, edge_out_in, node_in_in, node_out_in, biases_in, table_in,
-        out,
+        *refs,
+    ):
+        results, outs, refs = refs[0:6], refs[6:12], refs[12:]
+        (
         coarse, cot, edge_in, edge_out, node_in, node_out, biases, table, p0, p0_rim, xr, rim_r, vx, yr, means, lhs_rows, rows, e_all, e_sum, s_all, hn_all, u_all, g_all, xf,
-        gm, yb, back_blocks, back_rims, xb, rim_b, payload, core_slot, col_slots, plane_slots, total,
+        gm, yb, back_blocks, back_rims, xb, rim_b, payload, col_slots, plane_slots, total,
         load_sem, xf_s, xf_r, yf_s, yf_r, yb_s, yb_r, xb_s, xb_r,
-        core_s, core_r, col_s, col_r, plane_s, plane_r, cast_s, cast_r,
-    ):
+        col_s, col_r, plane_s, plane_r, cast_s, cast_r, save_sem,
+        ) = refs
+        g_coarse, g_edge_in, g_edge_out, g_node_in, g_node_out, g_biases = outs
+        saves = [pltpu.make_async_copy(src, dst, save_sem.at[i]) for i, (src, dst) in enumerate(zip(outs, results))]
         ix, iy, iz = lax.axis_index("gx"), lax.axis_index("gy"), lax.axis_index("gz")
         low = lax.rem(ix, Z_LOW)
         core = lax.rem(iy, CORES)
         layer = (iy // CORES) * Z_LOW + low
         on_core1 = core == 1
         is_root = on_core1 & (layer == 0)
-        is_leaf = on_core1 & (layer != 0)
+        member = layer * CORES + core
 
         def at_xz(d):
             return (lax.rem(ix + (d[0] + n_x), n_x), iy, lax.rem(iz + (d[1] + n_z), n_z))
@@ -214,13 +220,14 @@
         @pl.when(is_root)
         def _():
             for k in range(1, n_layers):
-                signal(in_column(k, 1))
+                for c in range(CORES):
+                    signal(in_column(k, c))
             for k in range(1, n_plane):
                 signal(in_plane(k))
 
         for c in loads[1:]:
             c.start()
-        expected = len(XZ) + len(STEPS) + jnp.where(is_leaf, 1, 0) + jnp.where(is_root, n_plane - 1, 0)
+        expected = len(XZ) + len(STEPS) + jnp.where(layer != 0, 1, 0) + jnp.where(is_root, n_plane - 1, 0)
 
         lane = iota((16, 128), 1)
         group, place = lane // 32, lane % 32
@@ -276,6 +283,7 @@
 
         m1 = mm(split(n_gathered), split(edge_out[...]))
         m1_wide = widen(m1)
+        n_back = split(transposed(n_gathered))
         m1_back = widen(transposed(m1))
         out_back = widen(transposed(node_out[...]))
         mix = split(jnp.concatenate([w_own, n_own, w_other], axis=0))
@@ -414,7 +422,7 @@
             hn = [line(vertex_rows(1, q, 0), vertex_rows(1, q, 1), t) for q in (0, 1)]
             put(11, x, hn[0] + b2_col)
             put(12, x, hn[1] - hn[0])
-            put(13, x, jnp.broadcast_to(nb_col, (16, 128)))
+        put(13, 0, jnp.broadcast_to(nb_col, (16, 128)))
         for side, (a, b, t, at) in enumerate(((-1, 0, float(L1[6]), float(T[6]) - 2.0), (1, 2, float(L1[1]), float(T[1]) + 2.0))):
             other = [
                 (line(vertex_rows(2, q, a), vertex_rows(2, q, b), t) + (at * col_x + (2 * q - 1.0) * col_y)) * LOG2E
@@ -428,6 +436,7 @@
                 return rows[pl.ds(128 * field + 8 * c + x, 1), :]
 
             other = [row(4, 0) + ly * row(4, 1)]
+            counted = count * row(13, 0)
             for x in range(8):
                 other.append(row(2, x) + ly * row(3, x))
             other.append(row(4, 2) + ly * row(4, 3))
@@ -452,7 +461,7 @@
                     decays = decay if decays is None else decays + decay
                 e_sum[x, c] = decays
                 s_all[c, :, 128 * x : 128 * x + 128] = LN2 * tops + (decays - count)
-                hn_all[c, :, 128 * x : 128 * x + 128] = row(11, x) + ly * row(12, x) + count * row(13, x)
+                hn_all[c, :, 128 * x : 128 * x + 128] = row(11, x) + ly * row(12, x) + counted
             return carry
 
         lax.fori_loop(0, 16, forward, 0)
@@ -596,14 +605,12 @@
         ]
         payload[...] = part + mm(split(jnp.concatenate(lefts, axis=1)), split(jnp.concatenate(rights, axis=1)), NT)
 
-        to_second = send(payload, core_slot, core_s, core_r, sibling)
         to_first = send(total, total, cast_s.at[0], cast_r, sibling)
-        slot = jnp.maximum(layer - 1, 0)
-        to_root = send(payload, col_slots.at[slot], col_s, col_r.at[slot], column_root)
-
-        @pl.when(core == 0)
-        def _():
-            to_second.start()
+        to_root = send(payload, col_slots.at[member], col_s, col_r.at[member], column_root)
+
+        @pl.when(jnp.logical_not(is_root))
+        def _():
+            to_root.start()
 
         zero = jnp.zeros((16, 128), F32)
         stacked = []
@@ -631,15 +638,6 @@
         for c in y_back:
             c.start()
 
-        @pl.when(on_core1)
-        def _():
-            to_second.wait_recv()
-            payload[...] = payload[...] + core_slot[...]
-
-        @pl.when(is_leaf)
-        def _():
-            to_root.start()
-
         edge_place = (place[0:8] < 2) | (place[0:8] == 17) | (place[0:8] == 18)
 
         def pack_back(block):
@@ -681,24 +679,12 @@
         @pl.when(is_root)
         def _():
             value = payload[...]
-            for k in range(n_layers - 1):
-                send(payload, col_slots.at[k], col_s, col_r.at[k], in_column(k + 1, 1)).wait_recv()
-                value = value + col_slots[k]
+            for k in range(CORES * n_layers):
+                if k != 1:
+                    send(payload, col_slots.at[k], col_s, col_r.at[k], sibling).wait_recv()
+                    value = value + col_slots[k]
             plane_slots[my_place] = value
             for c in to_plane:
-                c.start()
-
-        up_column = [send(total, total, cast_s.at[k], cast_r, in_column(k, 1)) for k in range(1, n_layers)]
-
-        @pl.when(is_root)
-        def _():
-            for k, c in enumerate(to_plane):
-                c.wait_recv()
-            value = plane_slots[0]
-            for k in range(1, n_plane):
-                value = value + plane_slots[k]
-            total[...] = value
-            for c in [to_first] + up_column:
                 c.start()
 
         for c in x_back:
@@ -714,40 +700,76 @@
             sides.append(unpack_back(value))
         level, sides = split(level), [split(v) for v in sides]
         value = mm_exact(level, maps[0], NT) + mm_exact(sides[0], maps[2], NT) + mm_exact(sides[1], maps[1], NT)
-        out[0:16, :] = value * jnp.where(group < 2, 0.25 / (1.0 + there[-1]), 0.25 / (1.0 + there[1]))
+        value = value * jnp.where(group < 2, 0.25 / (1.0 + there[-1]), 0.25 / (1.0 + there[1]))
+        for q in (0, 1):
+            for p in (0, 1):
+                g_coarse[:, p, q, :] = value[:, 32 * (2 * q + p) : 32 * (2 * q + p) + 32]
+        saves[0].start()
+
+        half = n_layers // 2
+        up_column = [send(total, total, cast_s.at[k], cast_r, in_column(k, 1)) for k in range(1, n_layers)]
+        is_helper = (core == 0) & (layer == 0)
+
+        @pl.when(is_root)
+        def _():
+            for k, c in enumerate(to_plane):
+                c.wait_recv()
+            value = plane_slots[0]
+            for k in range(1, n_plane):
+                value = value + plane_slots[k]
+            total[...] = value
+            for c in [to_first] + up_column[0 : half - 1]:
+                c.start()
 
         @pl.when(jnp.logical_not(is_root))
         def _():
             to_first.wait_recv()
 
-        @pl.when(is_leaf)
+        @pl.when(on_core1 & (layer != 0))
         def _():
             to_first.start()
 
-        out[16:32, :] = total[...]
-        out[32:48, 0:32] = node_in[...]
-        out[32:48, 32:48] = edge_out[...]
-        out[48:51, 0:16] = biases[...]
+        @pl.when(is_helper)
+        def _():
+            for c in up_column[half - 1 :]:
+                c.start()
+
+        sums = total[...] * factor
+        g_node_out[...] = sums[:, 0:16]
+        g_edge_in[...] = sums[:, 48:83]
+        back = mm(n_back, split(sums))
+        g_edge_out[...] = back[:, 16:32]
+        g_node_in[:, 0:16] = sums[:, 32:48]
+        g_node_in[:, 16:32] = mm(split(sums[:, 16:32]), split(edge_out[...]), NT) + sums[:, 85:86] * biases[1:2, :]
+        r, c = iota((8, 256), 0), iota((8, 256), 1)
+        pick = ones_where(((r == 0) & (c == 83)) | ((r == 1) & (c == 128 + 85)) | ((r == 2) & (c == 84))).astype(BF16)
+        g_biases[...] = exact_mm(pick, split(jnp.concatenate([sums, back], axis=1)), NT)[0:3, :]
+        for c in saves[1:]:
+            c.start()
 
         for c in x_sends + y_sends + y_back + x_back:
             c.wait_send()
 
-        @pl.when(core == 0)
-        def _():
-            to_second.wait_send()
-
         @pl.when(on_core1)
         def _():
             to_first.wait_send()
 
-        @pl.when(is_leaf)
+        @pl.when(jnp.logical_not(is_root))
         def _():
             to_root.wait_send()
 
         @pl.when(is_root)
         def _():
-            for c in to_plane + up_column:
+            for c in to_plane + up_column[0 : half - 1]:
                 c.wait_send()
+
+        @pl.when(is_helper)
+        def _():
+            for c in up_column[half - 1 :]:
+                c.wait_send()
+
+        for c in saves:
+            c.wait()
 
     block = pltpu.VMEM((16, 128), F32)
 
@@ -756,6 +778,7 @@
 
     dma = pltpu.SemaphoreType.DMA
     scratch = [
+        *(pltpu.VMEM(s, F32) for s in RESULTS),
         pltpu.VMEM((16, 2, 2, 32), F32),
         pltpu.VMEM((16, 8, 8, 128), F32),
         pltpu.VMEM((16, 35), F32),
@@ -787,20 +810,18 @@
         blocks(len(LEVEL)),
         pltpu.VMEM((len(ROUND), 8, 128), F32),
         block,
-        block,
-        blocks(n_layers - 1),
+        blocks(CORES * n_layers),
         blocks(n_plane),
         block,
         dma((8,)),
         dma((len(XZ),)), dma((len(XZ),)), dma((4,)), dma((4,)), dma((4,)), dma((4,)), dma((len(XZ),)), dma((len(XZ),)),
-        dma, dma, dma, dma((n_layers - 1,)), dma((n_plane,)), dma((n_plane,)), dma((n_layers,)), dma,
+        dma, dma((CORES * n_layers,)), dma((n_plane,)), dma((n_plane,)), dma((n_layers,)), dma, dma((6,)),
     ]
-    vmem = pl.BlockSpec(memory_space=pltpu.VMEM)
     return pl.pallas_call(
         kernel,
-        out_shape=jax.ShapeDtypeStruct((56, 128), F32),
+        out_shape=[jax.ShapeDtypeStruct(s, F32) for s in RESULTS],
         in_specs=[pl.BlockSpec(memory_space=pltpu.HBM)] * 8,
-        out_specs=vmem,
+        out_specs=[pl.BlockSpec(memory_space=pltpu.HBM)] * 6,
         scratch_shapes=scratch,
         compiler_params=pltpu.CompilerParams(
             collective_id=0, has_side_effects=True, vmem_limit_bytes=60 * 1024 * 1024
@@ -808,48 +829,26 @@
     )
 
 
-def make_finish(factor):
-    shapes = ((16, 2, 2, 32), (16, 35), (16, 16), (16, 32), (16, 16), (3, 16))
-
-    def kernel(packed, *refs):
-        outs, buffers, sem = refs[:6], refs[6:12], refs[12]
-        grad_coarse, g_edge_in, g_edge_out, g_node_in, g_node_out, g_biases = buffers
-        copies = [pltpu.make_async_copy(src, dst, sem.at[i]) for i, (src, dst) in enumerate(zip(buffers, outs))]
-        block = packed[0:16, :]
-        for q in (0, 1):
-            for p in (0, 1):
-                grad_coarse[:, p, q, :] = block[:, 32 * (2 * q + p) : 32 * (2 * q + p) + 32]
-        copies[0].start()
-        total = packed[16:32, :] * factor
-        g_node_out[...] = total[:, 0:16]
-        copies[4].start()
-        g_edge_in[...] = total[:, 48:83]
-        copies[1].start()
-        n_gathered, edge_out, b1_row = packed[32:48, 16:32], packed[32:48, 32:48], packed[49:50, 0:16]
-        eye = ones_where(iota((16, 16), 0) == iota((16, 16), 1)).astype(BF16)
-        n_back = exact_mm(eye, split(n_gathered), NT)
-        back = mm(split(n_back), split(total))
-        g_edge_out[...] = back[:, 16:32]
-        copies[2].start()
-        outer_in = total[:, 16:32]
-        g_node_in[:, 0:16] = total[:, 32:48]
-        g_node_in[:, 16:32] = mm(split(outer_in), split(edge_out), NT) + total[:, 85:86] * b1_row
-        copies[3].start()
-        rows = jnp.concatenate([total, back], axis=1)
-        r, c = iota((8, 256), 0), iota((8, 256), 1)
-        pick = ones_where(((r == 0) & (c == 83)) | ((r == 1) & (c == 128 + 85)) | ((r == 2) & (c == 84))).astype(BF16)
-        g_biases[...] = exact_mm(pick, split(rows), NT)[0:3, :]
-        copies[5].start()
-        for c in copies:
+def make_hand_over():
+    def kernel(*refs):
+        sources, outs, buffers, sem = refs[0:6], refs[6:12], refs[12:18], refs[18]
+        reads = [pltpu.make_async_copy(sources[i], buffers[i], sem.at[0, i]) for i in range(6)]
+        writes = [pltpu.make_async_copy(buffers[i], outs[i], sem.at[1, i]) for i in range(6)]
+        for c in reads:
+            c.start()
+        for read, write in zip(reads, writes):
+            read.wait()
+            write.start()
+        for c in writes:
             c.wait()
 
     return pl.pallas_call(
         kernel,
-        out_shape=[jax.ShapeDtypeStruct(s, F32) for s in shapes],
-        in_specs=[pl.BlockSpec(memory_space=pltpu.VMEM)],
+        out_shape=[jax.ShapeDtypeStruct(s, F32) for s in RESULTS],
+        in_specs=[pl.BlockSpec(memory_space=pltpu.HBM)] * 6,
         out_specs=[pl.BlockSpec(memory_space=pltpu.HBM)] * 6,
-        scratch_shapes=[pltpu.VMEM(s, F32) for s in shapes] + [pltpu.SemaphoreType.DMA((6,))],
-        compiler_params=pltpu.CompilerParams(vmem_limit_bytes=4 * 1024 * 1024),
+        scratch_shapes=[pltpu.VMEM(s, F32) for s in RESULTS] + [pltpu.SemaphoreType.DMA((2, 6))],
+        compiler_params=pltpu.CompilerParams(vmem_limit_bytes=60 * 1024 * 1024),
     )
 
 
@@ -859,10 +858,10 @@
 
     def on_device(coarse, cotangent, edge_in, edge_out, node_in, node_out, biases):
         nodes = cotangent.shape[1] * cotangent.shape[2] * cotangent.shape[3] * sizes[0] * sizes[1] * sizes[2]
-        packed = make_main(sizes)(
+        results = make_main(sizes, float(nodes) ** -0.5)(
             coarse, cotangent, edge_in, edge_out, node_in, node_out, biases, jnp.asarray(table)
         )
-        return tuple(make_finish(float(nodes) ** -0.5)(packed))
+        return tuple(make_hand_over()(*results))
 
     placed = (P(None, "gx", "gy", "gz"), P(None, "gx", "gy", "gz"), P(), P(), P(), P(), P())
     return jax.shard_map(

time: 49.7 us -> 48.7 us (0.980)
  local copies, waits for them, and re-layouts: 0.74 us -> 0 us
  Pallas kernels: 48.1 us -> 47.6 us
    unnamed x2 -> x0, local copies, waits for them, and re-layouts: 0.74 us -> none
where the time goes in v3:
time: 48.7 us; the launch traced here: 48.3 us
  Pallas kernels  47.6 us (98%)
  between operations  0.64 us (1%)
    pallas_call x1, Pallas kernels, on_device(): make_main(sizes, float(nodes) ** (-0.5))  46.2 us
    pallas_call x1, Pallas kernels, on_device(): return tuple(make_hand_over()(*results))  1.49 us

profile of v3, /device:TPU:1, one launch (start us, length us, event | category | flops | bytes accessed | tf_op | source)
XLA Modules:
  0.0 48.3 jit_solution(16095703935568916541)
XLA Ops:
  0.6 46.2 %shard_map.127 = (f32[16,2,2,32]{3,2,1,0:T(2,128)}, f32[16,35]{1,0:T(8,128)}, f32[16,16]{1,0:T(8,128)}, f32[16,32]{1,0:T(8,128)}, f32[16,16]{1,0:T(8,128)}, /*index=5*/f32[3,16]{1,0:T(4,128)}) custom-call(f32[16,2,2,32]{3,2,1,0:T(2,128)} %coarse_in.1, f32[16,8,8,128]{3,2,1,0:T(8,128)} %cot_in.1, f32[16,35]{1,0:T(8,128)} %edge_in_in.1, f32[16,16]{1,0:T(8,128)} %edge_out_in.1, ...), custom_call_target="tpu_custom_call" | custom-call | tf_op jit(solution)/shard_map/pallas_call | solution.py:861
  46.8 1.5 %shard_map.128 = (f32[16,2,2,32]{3,2,1,0:T(2,128)}, f32[16,35]{1,0:T(8,128)}, f32[16,16]{1,0:T(8,128)}, f32[16,32]{1,0:T(8,128)}, f32[16,16]{1,0:T(8,128)}, /*index=5*/f32[3,16]{1,0:T(4,128)}) custom-call(f32[16,2,2,32]{3,2,1,0:T(2,128)} %get-tuple-element.12.refs_0_, f32[16,35]{1,0:T(8,128)} %get-tuple-element.13.refs_1_, ...), custom_call_target="tpu_custom_call" | custom-call | tf_op jit(solution)/shard_map/pallas_call | solution.py:864

commit v4 on v3

--- a/solution.py
+++ b/solution.py
@@ -464,7 +464,7 @@
                 hn_all[c, :, 128 * x : 128 * x + 128] = row(11, x) + ly * row(12, x) + counted
             return carry
 
-        lax.fori_loop(0, 16, forward, 0)
+        lax.fori_loop(0, 16, forward, 0, unroll=2)
 
         outer_out = jnp.zeros((128, 128), F32)
         outer_in = jnp.zeros((128, 128), F32)
@@ -529,7 +529,7 @@
                 reduce(11 + 2 * k, [bz(2 + k, x) for x in range(8)])
             return carry
 
-        lax.fori_loop(0, 16, backward, 0)
+        lax.fori_loop(0, 16, backward, 0, unroll=2)
 
         def along_z(first, n, by):
             return mm(

time: 48.7 us -> 48.5 us (level)
  no operation moved by 1% of the time
where the time goes in v4:
time: 48.5 us; the launch traced here: 48.1 us
  Pallas kernels  47.4 us (98%)
  between operations  0.64 us (1%)
    pallas_call x1, Pallas kernels, on_device(): make_main(sizes, float(nodes) ** (-0.5))  45.9 us
    pallas_call x1, Pallas kernels, on_device(): return tuple(make_hand_over()(*results))  1.49 us

profile of v4, /device:TPU:1, one launch (start us, length us, event | category | flops | bytes accessed | tf_op | source)
XLA Modules:
  0.0 48.1 jit_solution(1396843175670167286)
XLA Ops:
  0.6 45.9 %shard_map.127 = (f32[16,2,2,32]{3,2,1,0:T(2,128)}, f32[16,35]{1,0:T(8,128)}, f32[16,16]{1,0:T(8,128)}, f32[16,32]{1,0:T(8,128)}, f32[16,16]{1,0:T(8,128)}, /*index=5*/f32[3,16]{1,0:T(4,128)}) custom-call(f32[16,2,2,32]{3,2,1,0:T(2,128)} %coarse_in.1, f32[16,8,8,128]{3,2,1,0:T(8,128)} %cot_in.1, f32[16,35]{1,0:T(8,128)} %edge_in_in.1, f32[16,16]{1,0:T(8,128)} %edge_out_in.1, ...), custom_call_target="tpu_custom_call" | custom-call | tf_op jit(solution)/shard_map/pallas_call | solution.py:861
  46.6 1.5 %shard_map.128 = (f32[16,2,2,32]{3,2,1,0:T(2,128)}, f32[16,35]{1,0:T(8,128)}, f32[16,16]{1,0:T(8,128)}, f32[16,32]{1,0:T(8,128)}, f32[16,16]{1,0:T(8,128)}, /*index=5*/f32[3,16]{1,0:T(4,128)}) custom-call(f32[16,2,2,32]{3,2,1,0:T(2,128)} %get-tuple-element.12.refs_0_, f32[16,35]{1,0:T(8,128)} %get-tuple-element.13.refs_1_, ...), custom_call_target="tpu_custom_call" | custom-call | tf_op jit(solution)/shard_map/pallas_call | solution.py:864

commit v5 on v4

--- a/solution.py
+++ b/solution.py
@@ -212,10 +212,10 @@
         ]
         loads[0].start()
         barrier = pltpu.get_barrier_semaphore()
+        for d in STEPS:
+            signal(at_y(d))
         for d in XZ:
             signal(at_xz(d))
-        for d in STEPS:
-            signal(at_y(d))
 
         @pl.when(is_root)
         def _():

time: 48.5 us -> 48.7 us (level)
  no operation moved by 1% of the time
where the time goes in v5:
time: 48.7 us; the launch traced here: 48.3 us
  Pallas kernels  47.7 us (98%)
  between operations  0.64 us (1%)
    pallas_call x1, Pallas kernels, on_device(): make_main(sizes, float(nodes) ** (-0.5))  46.2 us
    pallas_call x1, Pallas kernels, on_device(): return tuple(make_hand_over()(*results))  1.49 us

profile of v5, /device:TPU:1, one launch (start us, length us, event | category | flops | bytes accessed | tf_op | source)
XLA Modules:
  0.0 48.3 jit_solution(9769365883644564353)
XLA Ops:
  0.6 46.2 %shard_map.127 = (f32[16,2,2,32]{3,2,1,0:T(2,128)}, f32[16,35]{1,0:T(8,128)}, f32[16,16]{1,0:T(8,128)}, f32[16,32]{1,0:T(8,128)}, f32[16,16]{1,0:T(8,128)}, /*index=5*/f32[3,16]{1,0:T(4,128)}) custom-call(f32[16,2,2,32]{3,2,1,0:T(2,128)} %coarse_in.1, f32[16,8,8,128]{3,2,1,0:T(8,128)} %cot_in.1, f32[16,35]{1,0:T(8,128)} %edge_in_in.1, f32[16,16]{1,0:T(8,128)} %edge_out_in.1, ...), custom_call_target="tpu_custom_call" | custom-call | tf_op jit(solution)/shard_map/pallas_call | solution.py:861
  46.8 1.5 %shard_map.128 = (f32[16,2,2,32]{3,2,1,0:T(2,128)}, f32[16,35]{1,0:T(8,128)}, f32[16,16]{1,0:T(8,128)}, f32[16,32]{1,0:T(8,128)}, f32[16,16]{1,0:T(8,128)}, /*index=5*/f32[3,16]{1,0:T(4,128)}) custom-call(f32[16,2,2,32]{3,2,1,0:T(2,128)} %get-tuple-element.12.refs_0_, f32[16,35]{1,0:T(8,128)} %get-tuple-element.13.refs_1_, ...), custom_call_target="tpu_custom_call" | custom-call | tf_op jit(solution)/shard_map/pallas_call | solution.py:864
